TPU v7x, 512 devices: a whole 4x8x8 slice. The times are simulated.
512 devices in a mesh: inner: 32 (over z_hi, y), outer: 4 (over x), heads: 4 (over z_lo, core).
Axes of the slice: x: 4, y: 8, z: 8 (z_hi: 4, z_lo: 2; z = z_hi * 2 + z_lo), core: 2. Of those that a mesh axis runs over, the one named last changes fastest.
Arguments:
- q_raw: bfloat16 [16384, 64, 128], P(('inner', 'outer'), 'heads'), may hold values from -6 to 6
- k_raw: bfloat16 [16384, 8, 128], P(('inner', 'outer'), 'heads'), may hold values from -6 to 6
- values: bfloat16 [16384, 8, 128], P(('inner', 'outer'), 'heads'), may hold values from -6 to 6
- attn_out: bfloat16 [16384, 64, 128], P(('inner', 'outer'), 'heads'), may hold values from -1.796875 to 1.796875
- d_out: bfloat16 [16384, 64, 128], P(('inner', 'outer'), 'heads'), may hold values from -24 to 24
- lse: float32 [64, 16384], P('heads', ('inner', 'outer')), may hold values from 1 to 12
- q_gain: float32 [128], replicated, may hold values from 0.5 to 1.5
- k_gain: float32 [128], replicated, may hold values from 0.5 to 1.5
- span_order: int32 [256], replicated, may hold values from 0 to 255, as said below
Outputs:
- d_q_raw: bfloat16 [16384, 64, 128], P(('inner', 'outer'), 'heads')
- d_k_raw: bfloat16 [16384, 8, 128], P(('inner', 'outer'), 'heads')
- d_values: bfloat16 [16384, 8, 128], P(('inner', 'outer'), 'heads')
- d_q_gain: float32 [128], replicated
- d_k_gain: float32 [128], replicated
Inputs may be any that keep to these rules, and one draw needn't show every extreme that they name: `span_order`: for one whole number c0 of the draw, slots 2 b and 2 b + 1 hold spans c and 255 - c, in one order or the other for all b alike, with c = (b + c0) mod 128; so block b holds one early and one late span.
All inputs are finite; a program needn't handle non-finite values.
Results may differ from a plain program's by a relative error of at most 0.018.
The roundings to bfloat16 on the way count: a program that leaves them out, or rounds other values in their place, can miss the bound.
Values may be sent and summed in bfloat16 or wider, within the bound.
No kernel may reach another device: no remote copies, remote signals or barrier semaphores. Data moves between devices by JAX's collectives and lax.ppermute only.
A program may use at most 64 MiB of HBM per device.

v0:
```python
import jax
import jax.numpy as jnp
from jax import lax
from jax.sharding import PartitionSpec as P

WINDOW = 5


EPSILON = 1e-06


def from_behind(block, axis, distance):
    devices = range(lax.axis_size(axis))
    route = [((i - distance) % len(devices), i) for i in devices]
    return lax.ppermute(block, axis, route)


def normalize(raw_rows, gain_row):
    floats = raw_rows.astype(jnp.float32)
    inverse = lax.rsqrt(jnp.mean(floats * floats, axis=-1, keepdims=True) + EPSILON)
    unit_rows = floats * inverse
    return (unit_rows, inverse, (unit_rows * gain_row).astype(jnp.bfloat16))


def norm_backward(unit_rows, inverse, gain_row, gradient):
    scaled = gradient * gain_row
    projected = jnp.mean(scaled * unit_rows, axis=-1, keepdims=True)
    raw_grad = ((scaled - unit_rows * projected) * inverse).astype(jnp.bfloat16)
    return (raw_grad, jnp.sum(gradient * unit_rows, axis=(0, 1)))


def block_positions(span_order, device, tokens):
    half_rows = tokens // 2
    pair_ids = lax.dynamic_slice_in_dim(span_order, 2 * device, 2)
    offsets = jnp.arange(tokens, dtype=jnp.int32)
    starts = jnp.where(offsets < half_rows, pair_ids[0], pair_ids[1]) * half_rows
    return starts + offsets % half_rows


def per_device(q_raw, k_raw, values, attn_out, d_out, lse, q_gain, k_gain, span_order):
    tokens, q_heads, head_width = q_raw.shape
    kv_heads = k_raw.shape[1]
    members = q_heads // kv_heads
    score_scale = head_width ** (-0.5)
    cycle_size = lax.axis_size(("inner", "outer"))
    cycle_place = lax.axis_index(("inner", "outer"))
    unit_q, inverse_q, q_normed = normalize(q_raw, q_gain)
    unit_k, inverse_k, k_normed = normalize(k_raw, k_gain)
    queries = q_normed.reshape(tokens, kv_heads, members, head_width)
    grads_out = d_out.reshape(tokens, kv_heads, members, head_width)
    row_delta = jnp.sum(d_out.astype(jnp.float32) * attn_out.astype(jnp.float32), axis=-1)
    row_delta = row_delta.T.reshape(kv_heads, members, tokens)
    lse_rows = lse.reshape(kv_heads, members, tokens)
    query_pos = block_positions(span_order, cycle_place, tokens)
    home_block = jnp.stack([k_normed, values])

    def attend(kv_block, hop_step):
        source = (cycle_place - hop_step) % cycle_size
        key_pos = block_positions(span_order, source, tokens)
        visible = key_pos[None, :] <= query_pos[:, None]
        key_block = kv_block[0]
        value_block = kv_block[1]
        scores = (
            jnp.einsum("qhgd,khd->hgqk", queries, key_block, preferred_element_type=jnp.float32)
            * score_scale
        )
        probs = jnp.where(visible, jnp.exp(scores - lse_rows[..., None]), 0.0)
        probs_low = probs.astype(jnp.bfloat16)
        d_probs = jnp.einsum(
            "qhgd,khd->hgqk", grads_out, value_block, preferred_element_type=jnp.float32
        )
        d_scores = (probs * (d_probs - row_delta[..., None])).astype(jnp.bfloat16)
        d_query = (
            jnp.einsum("hgqk,khd->qhgd", d_scores, key_block, preferred_element_type=jnp.float32)
            * score_scale
        )
        d_key = (
            jnp.einsum("hgqk,qhgd->khd", d_scores, queries, preferred_element_type=jnp.float32)
            * score_scale
        )
        d_value = jnp.einsum(
            "hgqk,qhgd->khd", probs_low, grads_out, preferred_element_type=jnp.float32
        )
        return (d_query, jnp.stack([d_key, d_value]))

    d_query, travelling = attend(home_block, 0)
    moving = home_block
    for hop_step in range(1, WINDOW):
        moving = from_behind(moving, ("inner", "outer"), 1)
        more_query, pieces = attend(moving, hop_step)
        d_query = d_query + more_query
        travelling = (
            from_behind(travelling.astype(jnp.bfloat16), ("inner", "outer"), 1).astype(
                travelling.dtype
            )
            + pieces
        )
    travelling = from_behind(
        travelling.astype(jnp.bfloat16), ("inner", "outer"), 1 - WINDOW
    ).astype(travelling.dtype)
    d_q_normed = d_query.reshape(tokens, q_heads, head_width)
    d_q_raw, q_gain_part = norm_backward(unit_q, inverse_q, q_gain, d_q_normed)
    d_k_raw, k_gain_part = norm_backward(unit_k, inverse_k, k_gain, travelling[0])
    d_values = travelling[1].astype(jnp.bfloat16)
    d_q_gain, d_k_gain = lax.psum((q_gain_part, k_gain_part), ("inner", "outer", "heads"))
    return (d_q_raw, d_k_raw, d_values, d_q_gain, d_k_gain)


def solution(mesh):
    placed = (
        P(("inner", "outer"), "heads", None),
        P(("inner", "outer"), "heads", None),
        P(("inner", "outer"), "heads", None),
        P(("inner", "outer"), "heads", None),
        P(("inner", "outer"), "heads", None),
        P("heads", ("inner", "outer")),
        P(),
        P(),
        P(),
    )
    return jax.shard_map(
        per_device,
        mesh=mesh,
        in_specs=placed,
        out_specs=(
            P(("inner", "outer"), "heads", None),
            P(("inner", "outer"), "heads", None),
            P(("inner", "outer"), "heads", None),
            P(),
            P(),
        ),
        check_vma=False,
    )
```

profile of v0, /device:TPU:1, one launch (start us, length us, event | category | flops | bytes accessed | tf_op | source)
XLA Modules:
  0.0 220.1 jit_solution(18168475496431672183)
XLA Ops:
  0.7 1.4 fusion.59
  3.2 1.4 multiply_reduce_fusion
  6.0 1.3 multiply_add_fusion.5
  7.9 1.2 multiply_add_fusion.1
  9.8 1.2 multiply_add_fusion.2
  11.0 1.3 multiply_add_fusion.3
  12.2 1.3 multiply_add_fusion
  13.6 1.3 multiply_add_fusion.4
  19.0 4.0 %collective-permute-start.4 = (bf16[2,128,2,128]{3,1,2,0:T(8,128)(2,1)S(1)}, bf16[2,128,2,128]{3,1,2,0:T(8,128)(2,1)}, u32[]{:S(2)}, u32[]{:S(2)}) collective-permute-start(bf16[2,128,2,128]{3,1,2,0:T(8,128)(2,1)S(1)} %pad_maximum_fusion.1), channel_id=1, source_target_pairs={{508,0},{0,4},{4,8},{8,12},{12,16},{16,20},{20,24},{24,28},{28,32}... | collective-permute-start | bytes 393224 | tf_op jit(solution)/shard_map/ppermute | solution.py:15
  23.2 3.1 %collective-permute-start = (bf16[2,128,2,128]{3,1,2,0:T(8,128)(2,1)S(1)}, bf16[2,128,2,128]{3,1,2,0:T(8,128)(2,1)S(1)}, u32[]{:S(2)}, u32[]{:S(2)}) collective-permute-start(bf16[2,128,2,128]{3,1,2,0:T(8,128)(2,1)S(1)} %pad_maximum_fusion), channel_id=1, source_target_pairs={{508,0},{0,4},{4,8},{8,12},{12,16},{16,20},{20,24},{24,28},{28,32}... | collective-permute-start | bytes 393224 | tf_op jit(solution)/shard_map/ppermute | solution.py:15
  26.7 20.1 %collective-permute-done = bf16[2,128,2,128]{3,1,2,0:T(8,128)(2,1)S(1)} collective-permute-done((bf16[2,128,2,128]{3,1,2,0:T(8,128)(2,1)S(1)}, bf16[2,128,2,128]{3,1,2,0:T(8,128)(2,1)S(1)}, u32[]{:S(2)}, u32[]{:S(2)}) %collective-permute-start) | collective-permute-done | bytes 131104 | tf_op jit(solution)/shard_map/ppermute | solution.py:15
  47.8 1.2 copy.137
  49.0 1.4 fusion.42
  50.4 1.0 fusion.71
  51.4 1.9 collective-permute-start.5
  53.3 1.9 collective-permute-start.1
  55.3 1.3 convolution_add_fusion.3
  56.6 14.0 %collective-permute-done.1 = bf16[2,128,2,128]{3,1,2,0:T(8,128)(2,1)S(1)} collective-permute-done((bf16[2,128,2,128]{3,1,2,0:T(8,128)(2,1)S(1)}, bf16[2,128,2,128]{3,1,2,0:T(8,128)(2,1)S(1)}, u32[]{:S(2)}, u32[]{:S(2)}) %collective-permute-start.1) | collective-permute-done | bytes 131104 | tf_op jit(solution)/shard_map/ppermute | solution.py:15
  72.4 1.0 fusion.72
  73.4 1.9 collective-permute-start.6
  75.3 1.9 collective-permute-start.2
  77.6 12.4 %collective-permute-done.2 = bf16[2,128,2,128]{3,1,2,0:T(8,128)(2,1)S(1)} collective-permute-done((bf16[2,128,2,128]{3,1,2,0:T(8,128)(2,1)S(1)}, bf16[2,128,2,128]{3,1,2,0:T(8,128)(2,1)S(1)}, u32[]{:S(2)}, u32[]{:S(2)}) %collective-permute-start.2) | collective-permute-done | bytes 131104 | tf_op jit(solution)/shard_map/ppermute | solution.py:15
  91.0 1.2 copy.143
  92.2 1.4 fusion.46
  93.6 1.0 fusion.73
  94.6 1.9 collective-permute-start.7
  96.5 2.1 collective-permute-start.3
  98.7 1.3 convolution_add_fusion.1
  100.0 9.2 %collective-permute-done.3 = bf16[2,128,2,128]{3,1,2,0:T(8,128)(2,1)S(1)} collective-permute-done((bf16[2,128,2,128]{3,1,2,0:T(8,128)(2,1)S(1)}, bf16[2,128,2,128]{3,1,2,0:T(8,128)(2,1)S(1)}, u32[]{:S(2)}, u32[]{:S(2)}) %collective-permute-start.3) | collective-permute-done | bytes 131104 | tf_op jit(solution)/shard_map/ppermute | solution.py:15
  111.0 1.9 collective-permute-start.8
  114.6 1.4 fusion.57
  118.5 101.7 %all-reduce = (f32[128]{0:T(128)}, f32[128]{0:T(128)}) all-reduce(f32[128]{0:T(128)S(1)} %get-tuple-element.20, f32[128]{0:T(128)S(1)} %get-tuple-element.22), channel_id=1, replica_groups=mesh['inner'=32,'outer'=4,'heads'=4] {'inner','outer','heads'}, use_global_device_ids=true, to_apply=%region_6.7 | all-reduce | flops 256 | bytes 2048 | tf_op jit(solution)/shard_map/psum | solution.py:105
  (107 shorter events, 18.1 us)
Async XLA Ops:
  0.6 2.5 %copy-start = (bf16[128,16,128]{2,1,0:T(8,128)(2,1)S(1)}, bf16[128,16,128]{2,1,0:T(8,128)(2,1)}, u32[]{:S(2)}) copy-start(bf16[128,16,128]{2,1,0:T(8,128)(2,1)} %param.13) | copy-start | bytes 1572868
  2.2 0.8 copy-start.4
  3.1 11.7 %copy-start.1 = (bf16[128,16,128]{2,1,0:T(8,128)(2,1)S(1)}, bf16[128,16,128]{2,1,0:T(8,128)(2,1)}, u32[]{:S(2)}) copy-start(bf16[128,16,128]{2,1,0:T(8,128)(2,1)} %param.9) | copy-start | bytes 1572868
  4.7 0.7 copy-start.18
  13.5 1.3 copy-start.20
  15.2 0.8 copy-start.22
  17.1 0.8 copy-start.5
  19.0 31.3 %collective-permute-start.4 = (bf16[2,128,2,128]{3,1,2,0:T(8,128)(2,1)S(1)}, bf16[2,128,2,128]{3,1,2,0:T(8,128)(2,1)}, u32[]{:S(2)}, u32[]{:S(2)}) collective-permute-start(bf16[2,128,2,128]{3,1,2,0:T(8,128)(2,1)S(1)} %pad_maximum_fusion.1), channel_id=1, source_target_pairs={{508,0},{0,4},{4,8},{8,12},{12,16},{16,20},{20,24},{24,28},{28,32}... | collective-permute-start | bytes 393224 | tf_op jit(solution)/shard_map/ppermute | solution.py:15
  23.1 23.6 %copy-start.17 = (pred[128,128]{0,1:T(8,128)(4,1)S(1)}, pred[128,128]{0,1:T(8,128)(4,1)}, u32[]{:S(2)}) copy-start(pred[128,128]{0,1:T(8,128)(4,1)} %get-tuple-element.33) | copy-start | bytes 49156
  23.2 23.6 %copy-start.23 = (f32[16,128]{1,0:T(8,128)S(1)}, f32[16,128]{1,0:T(8,128)}, u32[]{:S(2)}) copy-start(f32[16,128]{1,0:T(8,128)} %param.14) | copy-start | bytes 24580
  23.2 23.6 %collective-permute-start = (bf16[2,128,2,128]{3,1,2,0:T(8,128)(2,1)S(1)}, bf16[2,128,2,128]{3,1,2,0:T(8,128)(2,1)S(1)}, u32[]{:S(2)}, u32[]{:S(2)}) collective-permute-start(bf16[2,128,2,128]{3,1,2,0:T(8,128)(2,1)S(1)} %pad_maximum_fusion), channel_id=1, source_target_pairs={{508,0},{0,4},{4,8},{8,12},{12,16},{16,20},{20,24},{24,28},{28,32}... | collective-permute-start | bytes 393224 | tf_op jit(solution)/shard_map/ppermute | solution.py:15
  46.8 0.7 copy-start.10
  50.4 2.9 %copy-start.11 = (bf16[2,128,2,128]{3,1,2,0:T(8,128)(2,1)S(1)}, bf16[2,128,2,128]{3,1,2,0:T(8,128)(2,1)}, u32[]{:S(2)}) copy-start(bf16[2,128,2,128]{3,1,2,0:T(8,128)(2,1)} %copy-done.10) | copy-start | bytes 393220
  51.4 19.2 %copy-start.16 = (pred[128,128]{0,1:T(8,128)(4,1)S(1)}, pred[128,128]{0,1:T(8,128)(4,1)}, u32[]{:S(2)}) copy-start(pred[128,128]{0,1:T(8,128)(4,1)} %get-tuple-element.34) | copy-start | bytes 49156
  51.4 19.2 %copy-start.24 = (f32[16,128]{1,0:T(8,128)S(1)}, f32[16,128]{1,0:T(8,128)}, u32[]{:S(2)}) copy-start(f32[16,128]{1,0:T(8,128)} %param.14) | copy-start | bytes 24580
  51.4 21.0 %collective-permute-start.5 = (bf16[2,128,2,128]{3,1,2,0:T(8,128)(2,1)S(1)}, bf16[2,128,2,128]{3,1,2,0:T(8,128)(2,1)}, u32[]{:S(2)}, u32[]{:S(2)}) collective-permute-start(bf16[2,128,2,128]{3,1,2,0:T(8,128)(2,1)S(1)} %fusion.71), channel_id=1, source_target_pairs={{508,0},{0,4},{4,8},{8,12},{12,16},{16,20},{20,24},{24,28},{28,32}... | collective-permute-start | bytes 393224 | tf_op jit(solution)/shard_map/ppermute | solution.py:15
  53.3 17.2 %collective-permute-start.1 = (bf16[2,128,2,128]{3,1,2,0:T(8,128)(2,1)S(1)}, bf16[2,128,2,128]{3,1,2,0:T(8,128)(2,1)S(1)}, u32[]{:S(2)}, u32[]{:S(2)}) collective-permute-start(bf16[2,128,2,128]{3,1,2,0:T(8,128)(2,1)S(1)} %copy-done.11), channel_id=1, source_target_pairs={{508,0},{0,4},{4,8},{8,12},{12,16},{16,20},{20,24},{24,28},{28,32}... | collective-permute-start | bytes 393224 | tf_op jit(solution)/shard_map/ppermute | solution.py:15
  72.0 5.2 %copy-start.2 = (f32[2,128,8,128]{3,1,2,0:T(8,128)S(1)}, f32[2,128,8,128]{3,1,2,0:T(8,128)}, u32[]{:S(2)}) copy-start(f32[2,128,8,128]{3,1,2,0:T(8,128)} %convolution_add_fusion.3) | copy-start | bytes 3145732
  72.4 2.9 %copy-start.7 = (bf16[2,128,2,128]{3,1,2,0:T(8,128)(2,1)S(1)}, bf16[2,128,2,128]{3,1,2,0:T(8,128)(2,1)}, u32[]{:S(2)}) copy-start(bf16[2,128,2,128]{3,1,2,0:T(8,128)(2,1)} %copy-done.6) | copy-start | bytes 393220
  73.4 16.6 %copy-start.15 = (pred[128,128]{0,1:T(8,128)(4,1)S(1)}, pred[128,128]{0,1:T(8,128)(4,1)}, u32[]{:S(2)}) copy-start(pred[128,128]{0,1:T(8,128)(4,1)} %get-tuple-element.35) | copy-start | bytes 49156
  73.4 16.6 %copy-start.25 = (f32[16,128]{1,0:T(8,128)S(1)}, f32[16,128]{1,0:T(8,128)}, u32[]{:S(2)}) copy-start(f32[16,128]{1,0:T(8,128)} %param.14) | copy-start | bytes 24580
  73.4 20.2 %collective-permute-start.6 = (bf16[2,128,2,128]{3,1,2,0:T(8,128)(2,1)S(1)}, bf16[2,128,2,128]{3,1,2,0:T(8,128)(2,1)}, u32[]{:S(2)}, u32[]{:S(2)}) collective-permute-start(bf16[2,128,2,128]{3,1,2,0:T(8,128)(2,1)S(1)} %fusion.72), channel_id=1, source_target_pairs={{508,0},{0,4},{4,8},{8,12},{12,16},{16,20},{20,24},{24,28},{28,32}... | collective-permute-start | bytes 393224 | tf_op jit(solution)/shard_map/ppermute | solution.py:15
  75.3 14.7 %collective-permute-start.2 = (bf16[2,128,2,128]{3,1,2,0:T(8,128)(2,1)S(1)}, bf16[2,128,2,128]{3,1,2,0:T(8,128)(2,1)S(1)}, u32[]{:S(2)}, u32[]{:S(2)}) collective-permute-start(bf16[2,128,2,128]{3,1,2,0:T(8,128)(2,1)S(1)} %copy-done.7), channel_id=1, source_target_pairs={{508,0},{0,4},{4,8},{8,12},{12,16},{16,20},{20,24},{24,28},{28,32}... | collective-permute-start | bytes 393224 | tf_op jit(solution)/shard_map/ppermute | solution.py:15
  90.0 0.7 copy-start.8
  93.6 2.9 %copy-start.9 = (bf16[2,128,2,128]{3,1,2,0:T(8,128)(2,1)S(1)}, bf16[2,128,2,128]{3,1,2,0:T(8,128)(2,1)}, u32[]{:S(2)}) copy-start(bf16[2,128,2,128]{3,1,2,0:T(8,128)(2,1)} %copy-done.8) | copy-start | bytes 393220
  94.6 14.6 %copy-start.14 = (pred[128,128]{0,1:T(8,128)(4,1)S(1)}, pred[128,128]{0,1:T(8,128)(4,1)}, u32[]{:S(2)}) copy-start(pred[128,128]{0,1:T(8,128)(4,1)} %get-tuple-element.32) | copy-start | bytes 49156
  94.6 14.6 %copy-start.26 = (f32[16,128]{1,0:T(8,128)S(1)}, f32[16,128]{1,0:T(8,128)}, u32[]{:S(2)}) copy-start(f32[16,128]{1,0:T(8,128)} %param.14) | copy-start | bytes 24580
  94.6 16.4 %collective-permute-start.7 = (bf16[2,128,2,128]{3,1,2,0:T(8,128)(2,1)S(1)}, bf16[2,128,2,128]{3,1,2,0:T(8,128)(2,1)S(1)}, u32[]{:S(2)}, u32[]{:S(2)}) collective-permute-start(bf16[2,128,2,128]{3,1,2,0:T(8,128)(2,1)S(1)} %fusion.73), channel_id=1, source_target_pairs={{508,0},{0,4},{4,8},{8,12},{12,16},{16,20},{20,24},{24,28},{28,32}... | collective-permute-start | bytes 393224 | tf_op jit(solution)/shard_map/ppermute | solution.py:15
  96.5 12.6 %collective-permute-start.3 = (bf16[2,128,2,128]{3,1,2,0:T(8,128)(2,1)S(1)}, bf16[2,128,2,128]{3,1,2,0:T(8,128)(2,1)S(1)}, u32[]{:S(2)}, u32[]{:S(2)}) collective-permute-start(bf16[2,128,2,128]{3,1,2,0:T(8,128)(2,1)S(1)} %copy-done.9), channel_id=1, source_target_pairs={{508,0},{0,4},{4,8},{8,12},{12,16},{16,20},{20,24},{24,28},{28,32}... | collective-permute-start | bytes 393224 | tf_op jit(solution)/shard_map/ppermute | solution.py:15
  110.6 2.4 %copy-start.3 = (f32[2,128,8,128]{3,1,2,0:T(8,128)S(1)}, f32[2,128,8,128]{3,1,2,0:T(8,128)}, u32[]{:S(2)}) copy-start(f32[2,128,8,128]{3,1,2,0:T(8,128)} %convolution_add_fusion.1) | copy-start | bytes 3145732
  111.0 2.0 copy-start.13
  111.0 5.7 %collective-permute-start.8 = (bf16[2,128,2,128]{3,1,2,0:T(8,128)(2,1)S(1)}, bf16[2,128,2,128]{3,1,2,0:T(8,128)(2,1)S(1)}, u32[]{:S(2)}, u32[]{:S(2)}) collective-permute-start(bf16[2,128,2,128]{3,1,2,0:T(8,128)(2,1)S(1)} %fusion.74), channel_id=1, source_target_pairs={{16,0},{20,4},{24,8},{28,12},{32,16},{36,20},{40,24},{44,28},{48,3... | collective-permute-start | bytes 393224 | tf_op jit(solution)/shard_map/ppermute | solution.py:15
  (4 other events, 2.7 us)
where the time goes:
time: 221 us; the launch traced here: 220 us
  blocking collectives  102 us (46%)
  waiting for transfers between devices  56.3 us (25%)
  starting transfers between devices  20.7 us (9%)
  other arithmetic  17.1 us (8%)
  matrix products  12.5 us (6%)
  local copies, waits for them, and re-layouts  10.4 us (5%)
    psum x1, blocking collectives, per_device(): lax.psum((q_gain_part, k_gain_part), ('inner', 'outer', 'heads'))  102 us
    ppermute x9, waiting for transfers between devices, from_behind(): return lax.ppermute(block, axis, route)  56.3 us
    ppermute x9, starting transfers between devices, from_behind(): return lax.ppermute(block, axis, route)  20.7 us
    add x6, other arithmetic, block_positions(): return starts + offsets % half_rows  7.57 us
  transfers between devices with their start and end apart: 9, of which 5 were waited for; matrix products, arithmetic and copies ran while one was open for 8% of the time, Pallas kernels for 0%

commit v1 on v0

v1 whole, which is shorter than its diff:
```python
import jax
import jax.numpy as jnp
import numpy as np
from jax import lax
from jax.experimental import pallas as pl
from jax.experimental.pallas import tpu as pltpu
from jax.sharding import PartitionSpec as P

F32 = jnp.float32
BF16 = jnp.bfloat16
EPSILON = 1e-06
TOK = 128
HALF = 64
KV = 2
MEM = 8
DH = 128
ROWS = HALF * MEM
SLOTS = 4
SCALE = DH ** (-0.5)
LOG2E = float(np.log2(np.e))
PAYLOAD = 2 * TOK * KV
EXTRA = 16
VMEM = pl.BlockSpec(memory_space=pltpu.VMEM)
SMEM = pl.BlockSpec(memory_space=pltpu.SMEM)
PARAMS = pltpu.CompilerParams(vmem_limit_bytes=32 * 1024 * 1024)


def dot_nt(a, b):
    return lax.dot_general(a, b, (((1,), (1,)), ((), ())), preferred_element_type=F32)


def dot_nn(a, b):
    return lax.dot_general(a, b, (((1,), (0,)), ((), ())), preferred_element_type=F32)


def dot_tn(a, b):
    return lax.dot_general(a, b, (((0,), (0,)), ((), ())), preferred_element_type=F32)


def unit_of(floats):
    inverse = lax.rsqrt(jnp.mean(floats * floats, axis=-1, keepdims=True) + EPSILON)
    return floats * inverse, inverse


def norm_backward(unit, inverse, gain, gradient):
    scaled = gradient * gain
    projected = jnp.mean(scaled * unit, axis=-1, keepdims=True)
    return (scaled - unit * projected) * inverse


def pair(key, value, query, grad_out, lse2, delta, mask=None):
    scores = dot_nt(key, query)
    probs = jnp.exp2(scores * (SCALE * LOG2E) - lse2)
    if mask is not None:
        probs = jnp.where(mask, probs, 0.0)
    d_probs = dot_nt(value, grad_out)
    d_scores = (probs * (d_probs - delta)).astype(BF16)
    d_value = dot_nn(probs.astype(BF16), grad_out)
    d_key = dot_nn(d_scores, query) * SCALE
    d_query = dot_tn(d_scores, key) * SCALE
    return d_query, d_key, d_value


def split(scratch, at, group):
    first = scratch[at, pl.ds(group, HALF, stride=KV), :].astype(BF16)
    second = scratch[at, pl.ds(TOK + group, HALF, stride=KV), :].astype(BF16)
    return first, second


def prep_kernel(info, q_raw, d_out, attn_out, lse2, k_raw, values, q_gain, k_gain,
                q_norm, grads_out, delta, d_query, d_local, k_part, keys):
    flip = info[0]
    flipped = flip == 1
    gain = q_gain[...]
    ones = jnp.ones((8, DH), F32)
    for group in range(KV):
        q_rows = q_raw[...].astype(F32)[:, group * MEM:(group + 1) * MEM, :]
        unit, _ = unit_of(q_rows.reshape(TOK * MEM, DH))
        normed = (unit * gain).astype(BF16)
        grads = d_out[...].astype(F32)[:, group * MEM:(group + 1) * MEM, :].reshape(TOK * MEM, DH)
        outs = attn_out[...].astype(F32)[:, group * MEM:(group + 1) * MEM, :].reshape(TOK * MEM, DH)
        row_delta = lax.dot_general(ones, grads * outs, (((1,), (1,)), ((), ())),
                                    precision=lax.Precision.HIGHEST, preferred_element_type=F32)
        grads = grads.astype(BF16)
        for half in range(2):
            rows = slice(half * ROWS, (half + 1) * ROWS)
            q_norm[group, half] = normed[rows]
            grads_out[group, half] = grads[rows]
            delta[group, half] = row_delta[0:1, rows]

    k_unit, _ = unit_of(k_raw[...].astype(F32))
    keys[0] = (k_unit * k_gain[...]).astype(BF16).astype(F32)
    keys[1] = values[...].astype(F32)
    key_at = lax.broadcasted_iota(jnp.int32, (HALF, ROWS), 0)
    query_at = lax.broadcasted_iota(jnp.int32, (HALF, ROWS), 1) // MEM
    mask = key_at <= query_at
    late = 1 - flip
    for group in range(KV):
        key = split(keys, 0, group)
        value = split(keys, 1, group)
        d_key = []
        d_value = []
        for half in range(2):
            dq, dk, dv = pair(key[half], value[half], q_norm[group, half], grads_out[group, half],
                              lse2[group, half], delta[group, half], mask)
            d_query[group, half] = dq
            d_key.append(dk)
            d_value.append(dv)
        early_key = jnp.where(flipped, key[1], key[0])
        early_value = jnp.where(flipped, value[1], value[0])
        dq, dk, dv = pair(early_key, early_value, q_norm[group, late], grads_out[group, late],
                          lse2[group, late], delta[group, late])
        d_query[group, late] += dq
        for half in range(2):
            here = flipped if half == 1 else jnp.logical_not(flipped)
            rows = pl.ds(half * TOK + group, HALF, stride=KV)
            d_local[0, rows, :] = d_key[half] + jnp.where(here, dk, 0.0)
            d_local[1, rows, :] = d_value[half] + jnp.where(here, dv, 0.0)
    k_part[...] = jnp.sum(d_local[0] * k_unit, axis=0, keepdims=True)


def build_kernel(info, k_own, v_own, k_behind, v_behind, out):
    place = info[1]
    for slot in range(SLOTS):
        own = slot > place
        out[slot, 0:TOK * KV] = jnp.where(own, k_own[...], k_behind[...])
        out[slot, TOK * KV:PAYLOAD] = jnp.where(own, v_own[...], v_behind[...])


def three_terms(row):
    high = row.astype(BF16).astype(F32)
    rest = row - high
    middle = rest.astype(BF16).astype(F32)
    return [high, middle, rest - middle]


def main_kernel(info, blocks, q_norm, grads_out, lse2, delta, d_query0, q_raw, q_gain, k_gain, k_part,
                d_q_raw, pieces, d_query, units, keys, vals, grads):
    flip = info[0]
    flipped = flip == 1
    late = 1 - flip
    for slot in range(SLOTS):
        unit, _ = unit_of(blocks[slot, 0:TOK * KV].astype(F32))
        units[slot] = unit
        keys[slot] = (unit * k_gain[...]).astype(BF16).astype(F32)
        vals[slot] = blocks[slot, TOK * KV:PAYLOAD].astype(F32)
    d_query[...] = d_query0[...]
    for group in range(KV):
        early_keys, early_values, late_keys, late_values = [], [], [], []
        for slot in range(SLOTS):
            key = split(keys, slot, group)
            value = split(vals, slot, group)
            early_keys.append(jnp.where(flipped, key[1], key[0]))
            late_keys.append(jnp.where(flipped, key[0], key[1]))
            early_values.append(jnp.where(flipped, value[1], value[0]))
            late_values.append(jnp.where(flipped, value[0], value[1]))
        dq, dk_all, dv_all = pair(jnp.concatenate(early_keys, 0), jnp.concatenate(early_values, 0),
                                  q_norm[group, late], grads_out[group, late],
                                  lse2[group, late], delta[group, late])
        d_query[group, late] += dq
        for slot in range(SLOTS):
            wraps = info[2 + slot] == 1
            half = jnp.where(wraps, late, flip)
            dq, dk, dv = pair(jnp.where(wraps, late_keys[slot], early_keys[slot]),
                              jnp.where(wraps, late_values[slot], early_values[slot]),
                              q_norm[group, half], grads_out[group, half],
                              lse2[group, half], delta[group, half])
            d_query[group, half] += dq
            span = slice(slot * HALF, (slot + 1) * HALF)
            for which, everyone, rest in ((0, dk_all[span], dk), (1, dv_all[span], dv)):
                of_early = everyone + jnp.where(wraps, 0.0, rest)
                of_late = jnp.where(wraps, rest, 0.0)
                at = slot * 2 + which
                grads[at, pl.ds(group, HALF, stride=KV), :] = jnp.where(flipped, of_late, of_early)
                grads[at, pl.ds(TOK + group, HALF, stride=KV), :] = jnp.where(flipped, of_early, of_late)

    k_sum = k_part[...]
    for slot in range(SLOTS):
        k_sum += jnp.sum(grads[2 * slot] * units[slot], axis=0, keepdims=True)
        pieces[slot, 0:TOK * KV] = grads[2 * slot].astype(BF16)
        pieces[slot, TOK * KV:PAYLOAD] = grads[2 * slot + 1].astype(BF16)

    q_sum = jnp.zeros((1, DH), F32)
    gain = q_gain[...]
    for half in range(2):
        tokens = slice(half * HALF, (half + 1) * HALF)
        raw = q_raw[tokens].astype(F32)
        made = []
        for group in range(KV):
            rows = raw[:, group * MEM:(group + 1) * MEM, :].reshape(ROWS, DH)
            unit, inverse = unit_of(rows)
            gradient = d_query[group, half]
            q_sum += jnp.sum(gradient * unit, axis=0, keepdims=True)
            made.append(norm_backward(unit, inverse, gain, gradient).reshape(HALF, MEM, DH))
        d_q_raw[tokens] = jnp.concatenate(made, axis=1).astype(BF16)

    terms = three_terms(q_sum) + three_terms(k_sum) + [jnp.zeros((EXTRA - 6, DH), F32)]
    extra = jnp.concatenate(terms, axis=0).astype(BF16)
    for slot in range(SLOTS):
        pieces[slot, PAYLOAD:PAYLOAD + EXTRA] = extra


def sum_kernel(info, pieces, d_local, own, behind, gains):
    place = info[1]
    total = jnp.concatenate([d_local[0], d_local[1]], axis=0)
    others = jnp.zeros((PAYLOAD, DH), F32)
    extra = jnp.zeros((EXTRA, DH), F32)
    for slot in range(SLOTS):
        piece = pieces[slot, 0:PAYLOAD].astype(F32)
        ahead = slot > place
        total += jnp.where(ahead, piece, 0.0)
        others += jnp.where(ahead, 0.0, piece)
        extra += pieces[slot, PAYLOAD:PAYLOAD + EXTRA].astype(F32)
    own[...] = total
    behind[...] = others.astype(BF16)
    both = jnp.concatenate([jnp.sum(extra[0:3], axis=0, keepdims=True), jnp.sum(extra[3:6], axis=0, keepdims=True)], axis=0)
    for place in range(gains.shape[0]):
        gains[place] = both


def relay_kernel(gathered, spread):
    both = jnp.sum(gathered[...], axis=0)
    for place in range(spread.shape[0]):
        spread[place] = both


def last_kernel(own, arrived, k_raw, k_gain, gathered, d_k_raw, d_values, q_sum, k_sum):
    total = own[...] + arrived[...].astype(F32)
    unit, inverse = unit_of(k_raw[...].astype(F32))
    d_k_raw[...] = norm_backward(unit, inverse, k_gain[...], total[0:TOK * KV]).astype(BF16)
    d_values[...] = total[TOK * KV:PAYLOAD].astype(BF16)
    both = jnp.sum(gathered[...], axis=0)
    q_sum[...] = both[0:1]
    k_sum[...] = both[1:2]


def call(kernel, outs, specs, scratch=(), flops=0, size=0):
    return pl.pallas_call(
        kernel,
        out_shape=[jax.ShapeDtypeStruct(*o) for o in outs],
        in_specs=specs,
        out_specs=[VMEM] * len(outs),
        scratch_shapes=list(scratch),
        compiler_params=PARAMS,
        cost_estimate=pl.CostEstimate(flops=flops, bytes_accessed=size, transcendentals=0),
    )


def step(block, axes, distance):
    size = lax.axis_size(axes)
    return lax.ppermute(block, axes, [((i - distance) % size, i) for i in range(size)])


def per_device(q_raw, k_raw, values, attn_out, d_out, lse, q_gain, k_gain, span_order):
    k_own = k_raw.reshape(TOK * KV, DH)
    v_own = values.reshape(TOK * KV, DH)
    k_behind = step(k_own, ("zh", "y"), 1)
    v_behind = step(v_own, ("zh", "y"), 1)

    place = lax.axis_index("x")
    block = lax.axis_index(("zh", "y", "x"))
    spans = lax.dynamic_slice_in_dim(span_order, 2 * block, 2)
    flip = (spans[0] > spans[1]).astype(jnp.int32)
    early = jnp.minimum(spans[0], spans[1])
    hops = (place - jnp.arange(SLOTS, dtype=jnp.int32) - 1) % SLOTS + 1
    info = jnp.concatenate([jnp.stack([flip, place]), (hops > early).astype(jnp.int32)])
    q_gain = q_gain.reshape(1, DH)
    k_gain = k_gain.reshape(1, DH)
    lse2 = (lse * LOG2E).reshape(KV, MEM, TOK).transpose(0, 2, 1).reshape(KV, 2, 1, ROWS)

    q_norm, grads_out, delta, d_query0, d_local, k_part = call(
        prep_kernel,
        [((KV, 2, ROWS, DH), BF16), ((KV, 2, ROWS, DH), BF16), ((KV, 2, 1, ROWS), F32),
         ((KV, 2, ROWS, DH), F32), ((2, TOK * KV, DH), F32), ((1, DH), F32)],
        [SMEM] + [VMEM] * 8,
        [pltpu.VMEM((2, TOK * KV, DH), F32)],
        flops=int(6e9), size=1 << 22,
    )(info, q_raw, d_out, attn_out, lse2, k_own, v_own, q_gain, k_gain)

    (blocks,) = call(build_kernel, [((SLOTS, PAYLOAD, DH), BF16)], [SMEM] + [VMEM] * 4)(
        info, k_own, v_own, k_behind, v_behind)
    blocks = lax.all_to_all(blocks, "x", 0, 0)
    d_q_raw, pieces = call(
        main_kernel,
        [((TOK, KV * MEM, DH), BF16), ((SLOTS, PAYLOAD + EXTRA, DH), BF16)],
        [SMEM] + [VMEM] * 10,
        [pltpu.VMEM((KV, 2, ROWS, DH), F32), pltpu.VMEM((SLOTS, TOK * KV, DH), F32),
         pltpu.VMEM((SLOTS, TOK * KV, DH), F32), pltpu.VMEM((SLOTS, TOK * KV, DH), F32),
         pltpu.VMEM((2 * SLOTS, TOK * KV, DH), F32)],
    )(info, blocks, q_norm, grads_out, lse2, delta, d_query0, q_raw, q_gain, k_gain, k_part)
    pieces = lax.all_to_all(pieces, "x", 0, 0)
    own, behind, gains = call(
        sum_kernel,
        [((PAYLOAD, DH), F32), ((PAYLOAD, DH), BF16), ((lax.axis_size("y"), 2, DH), F32)],
        [SMEM] + [VMEM] * 2,
    )(info, pieces, d_local)
    arrived = step(behind, ("zh", "y"), -1)
    gains = lax.all_to_all(gains, "y", 0, 0)
    others = ("zh", "zl", "c")
    (gains,) = call(relay_kernel, [((lax.axis_size(others), 2, DH), F32)], [VMEM])(gains)
    gains = lax.all_to_all(gains, others, 0, 0)
    d_k_raw, d_values, d_q_gain, d_k_gain = call(
        last_kernel,
        [((TOK * KV, DH), BF16), ((TOK * KV, DH), BF16), ((1, DH), F32), ((1, DH), F32)],
        [VMEM] * 5,
    )(own, arrived, k_own, k_gain, gains)
    return (d_q_raw, d_k_raw.reshape(TOK, KV, DH), d_values.reshape(TOK, KV, DH),
            d_q_gain.reshape(DH), d_k_gain.reshape(DH))


def solution(mesh):
    devices = np.asarray(mesh.devices).reshape(4, 8, 4, 2, 2)
    mesh = jax.sharding.Mesh(devices, ("zh", "y", "x", "zl", "c"))
    rows = ("zh", "y", "x")
    heads = ("zl", "c")
    placed = P(rows, heads, None)
    return jax.shard_map(
        per_device,
        mesh=mesh,
        in_specs=(placed,) * 5 + (P(heads, rows), P(), P(), P()),
        out_specs=(placed,) * 3 + (P(), P()),
        check_vma=False,
    )
```

time: 221 us -> 82.9 us (0.38)
  blocking collectives: 102 us -> 37.7 us
  waiting for transfers between devices: 56.3 us -> 8.7 us
  other arithmetic: 17.1 us -> 0.1 us
  matrix products: 12.5 us -> 0 us
  Pallas kernels: 0 us -> 11.4 us
  starting transfers between devices: 20.7 us -> 15 us
  local copies, waits for them, and re-layouts: 10.4 us -> 6.05 us
    psum x1 -> x0, blocking collectives: 102 us -> none  [per_device(): lax.psum((q_gain_part, k_gain_part), ('inner', 'outer', 'heads'))]
    ppermute x9 -> x3, waiting for transfers between devices: 56.3 us -> 8.29 us  [step(): lax.ppermute(block, axes, [((i - distance) % size, i) for i in range(size)])]
    all_to_all x0 -> x3, blocking collectives: none -> 37.7 us  [the longest x1 18.2 us: per_device(): gains = lax.all_to_all(gains, others, 0, 0)]
    dot_general x25 -> x0, matrix products: 12.5 us -> none  [the longest x5 3.8 us: attend(): jnp.einsum('hgqk,qhgd->khd', d_scores, queries, preferred_element_type=jn...]
    pallas_call x0 -> x6, Pallas kernels: none -> 11.4 us  [the longest x1 5.06 us: per_device(): call(main_kernel, [((TOK, KV * MEM, DH), BF16), ((SLOTS, PAYLOAD + EXTRA,...]
    ppermute x9 -> x3, starting transfers between devices: 20.7 us -> 10.8 us  [step(): lax.ppermute(block, axes, [((i - distance) % size, i) for i in range(size)])]
    add x6 -> x0, other arithmetic: 7.57 us -> none  [block_positions(): return starts + offsets % half_rows]
    convert_element_type x6 -> x1, other arithmetic: 4.49 us -> 0.01 us  [per_device(): (hops > early).astype(jnp.int32)]
  transfers between devices with their start and end apart: 9 -> 4, of which waited for: 5 -> 3; matrix products, arithmetic and copies ran while one was open for 8% -> 1% of each run, Pallas kernels for 0% -> 4%
where the time goes in v1:
time: 82.9 us; the launch traced here: 82.3 us
  blocking collectives  37.7 us (45%)
  starting transfers between devices  15 us (18%)
  Pallas kernels  11.4 us (14%)
  waiting for transfers between devices  8.7 us (10%)
  local copies, waits for them, and re-layouts  6.05 us (7%)
  between operations  3.36 us (4%)
    all_to_all x1, blocking collectives, per_device(): gains = lax.all_to_all(gains, others, 0, 0)  18.2 us
    ppermute x3, starting transfers between devices, step(): lax.ppermute(block, axes, [((i - distance) % size, i) for i in range(size)])  10.8 us
    all_to_all x1, blocking collectives, per_device(): pieces = lax.all_to_all(pieces, 'x', 0, 0)  10.6 us
    all_to_all x1, blocking collectives, per_device(): gains = lax.all_to_all(gains, 'y', 0, 0)  8.93 us
    ppermute x3, waiting for transfers between devices, step(): lax.ppermute(block, axes, [((i - distance) % size, i) for i in range(size)])  8.29 us
    unnamed x32, local copies, waits for them, and re-layouts  5.16 us
    pallas_call x1, Pallas kernels, per_device(): call(main_kernel, [((TOK, KV * MEM, DH), BF16), ((SLOTS, PAYLOAD + EXTRA,...  5.06 us
    all_to_all x1, starting transfers between devices, per_device(): blocks = lax.all_to_all(blocks, 'x', 0, 0)  4.14 us
  transfers between devices with their start and end apart: 4, of which 3 were waited for; matrix products, arithmetic and copies ran while one was open for 1% of the time, Pallas kernels for 4%

profile of v1, /device:TPU:1, one launch (start us, length us, event | category | flops | bytes accessed | tf_op | source)
XLA Modules:
  0.0 82.3 jit_solution(10406520503889397916)
XLA Ops:
  0.6 4.0 %collective-permute-start = (bf16[256,128]{1,0:T(8,128)(2,1)}, bf16[256,128]{1,0:T(8,128)(2,1)S(1)}, u32[]{:S(2)}, u32[]{:S(2)}) collective-permute-start(bf16[256,128]{1,0:T(8,128)(2,1)} %bitcast.13), channel_id=1, source_target_pairs={{496,0},{0,16},{16,32},{32,48},{48,64},{64,80},{80,96},{96,112},{1... | collective-permute-start | bytes 196616 | tf_op jit(solution)/shard_map/ppermute | solution.py:251
  4.7 3.2 %collective-permute-start.1 = (bf16[256,128]{1,0:T(8,128)(2,1)}, bf16[256,128]{1,0:T(8,128)(2,1)S(1)}, u32[]{:S(2)}, u32[]{:S(2)}) collective-permute-start(bf16[256,128]{1,0:T(8,128)(2,1)} %bitcast.17), channel_id=1, source_target_pairs={{496,0},{0,16},{16,32},{32,48},{48,64},{64,80},{80,96},{96,112},{1... | collective-permute-start | bytes 196616 | tf_op jit(solution)/shard_map/ppermute | solution.py:251
  7.9 0.7 copy-done.15
  8.6 0.1 dynamic_slice.3
  8.7 0.6 fusion.2
  11.9 0.1 copy.15
  12.0 0.1 reshape.54.lse2
  12.1 0.1 pad_add_fusion.info
  12.2 5.4 %collective-permute-done.k_behind = bf16[256,128]{1,0:T(8,128)(2,1)S(1)} collective-permute-done((bf16[256,128]{1,0:T(8,128)(2,1)}, bf16[256,128]{1,0:T(8,128)(2,1)S(1)}, u32[]{:S(2)}, u32[]{:S(2)}) %collective-permute-start) | collective-permute-done | bytes 65568 | tf_op jit(solution)/shard_map/ppermute | solution.py:251
  17.6 2.9 %collective-permute-done.1.v_behind = bf16[256,128]{1,0:T(8,128)(2,1)S(1)} collective-permute-done((bf16[256,128]{1,0:T(8,128)(2,1)}, bf16[256,128]{1,0:T(8,128)(2,1)S(1)}, u32[]{:S(2)}, u32[]{:S(2)}) %collective-permute-start.1) | collective-permute-done | bytes 65568 | tf_op jit(solution)/shard_map/ppermute | solution.py:251
  20.5 1.5 %shard_map.128 = bf16[4,512,128]{2,1,0:T(8,128)(2,1)} custom-call(s32[6]{0:T(128)S(1)} %pad_add_fusion.info, bf16[256,128]{1,0:T(8,128)(2,1)S(1)} %bitcast.14, bf16[256,128]{1,0:T(8,128)(2,1)S(1)} %bitcast.18, bf16[256,128]{1,0:T(8,128)(2,1)S(1)} %collective-permute-done.k_behind, bf16[256,128]{1,0:T(8,128)(2,1)S(1)} %collective-permute-done.1.v_behind), custom_call_target="tpu_custom_call" | custom-call | tf_op jit(solution)/shard_map/pallas_call | solution.py:280
  22.0 0.5 copy-done.3
  22.5 4.1 %all-to-all-start = ((bf16[4,512,128]{2,1,0:T(8,128)(2,1)}), bf16[4,512,128]{2,1,0:T(8,128)(2,1)S(1)}, u32[]{:S(2)}, u32[]{:S(2)}) async-start(bf16[4,512,128]{2,1,0:T(8,128)(2,1)} %shard_map.128), calls=%async_computation | async-start | bytes 1048576 | tf_op jit(solution)/shard_map/all_to_all | solution.py:282
  26.7 0.6 copy-done.4
  27.3 0.0 copy-done.6
  27.3 0.0 copy-done.8
  27.3 1.0 %copy-done.12 = bf16[128,16,128]{2,1,0:T(8,128)(2,1)S(1)} copy-done((bf16[128,16,128]{2,1,0:T(8,128)(2,1)S(1)}, bf16[128,16,128]{2,1,0:T(8,128)(2,1)}, u32[]{:S(2)}) %copy-start.12) | copy-done | bytes 524312
  28.4 1.0 %copy-done.13 = bf16[128,16,128]{2,1,0:T(8,128)(2,1)S(1)} copy-done((bf16[128,16,128]{2,1,0:T(8,128)(2,1)S(1)}, bf16[128,16,128]{2,1,0:T(8,128)(2,1)}, u32[]{:S(2)}) %copy-start.13) | copy-done | bytes 524312
  29.4 3.3 %shard_map.129 = (bf16[2,2,512,128]{3,2,1,0:T(8,128)(2,1)S(1)}, bf16[2,2,512,128]{3,2,1,0:T(8,128)(2,1)S(1)}, f32[2,2,1,512]{3,2,1,0:T(1,128)S(1)}, f32[2,2,512,...) custom-call(s32[6]{0:T(128)S(1)} %copy-done.4, bf16[128,16,128]{2,1,0:T(8,128)(2,1)S(1)} %copy-done, ...), custom_call_target="tpu_custom_call" | custom-call | flops 6000000000 | bytes 4194304 | tf_op jit(solution)/shard_map/pallas_call | solution.py:271
  32.7 0.5 copy-done.10
  33.2 0.4 all-to-all-done.blocks
  33.6 0.6 copy-done.11
  34.3 0.0 copy-done.5
  34.3 0.0 copy-done.7
  34.3 0.0 copy-done.9
  34.3 5.1 %shard_map.130 = (bf16[128,16,128]{2,1,0:T(8,128)(2,1)}, bf16[4,528,128]{2,1,0:T(8,128)(2,1)S(1)}) custom-call(s32[6]{0:T(128)S(1)} %copy-done.5, bf16[4,512,128]{2,1,0:T(8,128)(2,1)S(1)} %all-to-all-done.blocks, bf16[2,2,512,128]{3,2,1,0:T(8,128)(2,1)S(1)} %get-tuple-element.20.q_norm, bf16[2,2,512,128]{3,2,1,0:T(8,128)(2,1)S(1)} %get-tuple-element.21.grads_out, ...), custom_call_target="tpu_custom_call" | custom-call | tf_op jit(solution)/shard_map/pallas_call | solution.py:283
  39.4 10.6 %all_to_all.20.pieces = bf16[4,528,128]{2,1,0:T(8,128)(2,1)S(1)} all-to-all(bf16[4,528,128]{2,1,0:T(8,128)(2,1)S(1)} %get-tuple-element.26), channel_id=1, replica_groups=mesh['zh'=4,'y'=8,'x'=4,'zl'=2,'c'=2] {'x'}, dimensions={0} | all-to-all | bytes 1081344 | tf_op jit(solution)/shard_map/all_to_all | solution.py:291
  50.0 0.8 shard_map.131
  50.8 3.6 %collective-permute-start.2 = (bf16[512,128]{1,0:T(8,128)(2,1)S(1)}, bf16[512,128]{1,0:T(8,128)(2,1)S(1)}, u32[]{:S(2)}, u32[]{:S(2)}) collective-permute-start(bf16[512,128]{1,0:T(8,128)(2,1)S(1)} %get-tuple-element.29), channel_id=1, source_target_pairs={{16,0},{32,16},{48,32},{64,48},{80,64},{96,80},{112,96},{128,112},... | collective-permute-start | bytes 393224 | tf_op jit(solution)/shard_map/ppermute | solution.py:251
  54.4 8.9 %all_to_all.21.gathered = f32[8,2,128]{2,1,0:T(2,128)S(1)} all-to-all(f32[8,2,128]{2,1,0:T(2,128)S(1)} %get-tuple-element.30), channel_id=1, replica_groups=mesh['zh'=4,'y'=8,'x'=4,'zl'=2,'c'=2] {'y'}, dimensions={0} | all-to-all | bytes 16384 | tf_op jit(solution)/shard_map/all_to_all | solution.py:298
  63.3 18.2 %all_to_all.22.gathered = f32[16,2,128]{2,1,0:T(2,128)S(1)} all-to-all(f32[16,2,128]{2,1,0:T(2,128)S(1)} %shard_map.132), channel_id=1, replica_groups=mesh['zh'=4,'y'=8,'x'=4,'zl'=2,'c'=2] {'zh','zl','c'}, dimensions={0} | all-to-all | bytes 32768 | tf_op jit(solution)/shard_map/all_to_all | solution.py:301
  81.5 0.8 %shard_map.133 = (bf16[256,128]{1,0:T(8,128)(2,1)}, bf16[256,128]{1,0:T(8,128)(2,1)}, f32[1,128]{1,0:T(1,128)}, f32[1,128]{1,0:T(1,128)}) custom-call(f32[512,128]{1,0:T(8,128)S(1)} %get-tuple-element.28.own, bf16[512,128]{1,0:T(8,128)(2,1)S(1)} %collective-permute-done.2.arrived, bf16[256,128]{1,0:T(8,128)(2,1)S(1)} %bitcast.16, f32[1,128]{1,0:T(1,128)S(1)} %bitcast.22, ...), custom_call_target="tpu_custom_call" | custom-call | tf_op jit(solution)/shard_map/pallas_call | solution.py:302
  (24 shorter events, 0.1 us)
Async XLA Ops:
  0.6 16.9 %collective-permute-start = (bf16[256,128]{1,0:T(8,128)(2,1)}, bf16[256,128]{1,0:T(8,128)(2,1)S(1)}, u32[]{:S(2)}, u32[]{:S(2)}) collective-permute-start(bf16[256,128]{1,0:T(8,128)(2,1)} %bitcast.13), channel_id=1, source_target_pairs={{496,0},{0,16},{16,32},{32,48},{48,64},{64,80},{80,96},{96,112},{1... | collective-permute-start | bytes 196616 | tf_op jit(solution)/shard_map/ppermute | solution.py:251
  4.7 15.8 %collective-permute-start.1 = (bf16[256,128]{1,0:T(8,128)(2,1)}, bf16[256,128]{1,0:T(8,128)(2,1)S(1)}, u32[]{:S(2)}, u32[]{:S(2)}) collective-permute-start(bf16[256,128]{1,0:T(8,128)(2,1)} %bitcast.17), channel_id=1, source_target_pairs={{496,0},{0,16},{16,32},{32,48},{48,64},{64,80},{80,96},{96,112},{1... | collective-permute-start | bytes 196616 | tf_op jit(solution)/shard_map/ppermute | solution.py:251
  7.9 0.7 copy-start.15
  8.7 3.2 %copy-start.14 = (f32[16,128]{1,0:T(8,128)S(1)}, f32[16,128]{1,0:T(8,128)}, u32[]{:S(2)}) copy-start(f32[16,128]{1,0:T(8,128)} %param.14) | copy-start | bytes 24580
  12.0 8.5 %copy-start.1 = (bf16[128,2,128]{2,1,0:T(2,128)(2,1)S(1)}, bf16[128,2,128]{2,1,0:T(2,128)(2,1)}, u32[]{:S(2)}) copy-start(bf16[128,2,128]{2,1,0:T(2,128)(2,1)} %param.10) | copy-start | bytes 196612
  12.0 8.5 %copy-start.2 = (bf16[128,2,128]{2,1,0:T(2,128)(2,1)S(1)}, bf16[128,2,128]{2,1,0:T(2,128)(2,1)}, u32[]{:S(2)}) copy-start(bf16[128,2,128]{2,1,0:T(2,128)(2,1)} %param.11) | copy-start | bytes 196612
  22.0 0.5 copy-start.3
  22.5 4.2 %copy-start = (bf16[128,16,128]{2,1,0:T(8,128)(2,1)S(1)}, bf16[128,16,128]{2,1,0:T(8,128)(2,1)}, u32[]{:S(2)}) copy-start(bf16[128,16,128]{2,1,0:T(8,128)(2,1)} %q_raw.3) | copy-start | bytes 1572868
  22.5 11.1 %all-to-all-start = ((bf16[4,512,128]{2,1,0:T(8,128)(2,1)}), bf16[4,512,128]{2,1,0:T(8,128)(2,1)S(1)}, u32[]{:S(2)}, u32[]{:S(2)}) async-start(bf16[4,512,128]{2,1,0:T(8,128)(2,1)} %shard_map.128), calls=%async_computation | async-start | bytes 1048576 | tf_op jit(solution)/shard_map/all_to_all | solution.py:282
  26.6 0.7 copy-start.4
  26.6 0.7 copy-start.6
  26.6 0.7 copy-start.8
  27.3 1.0 %copy-start.12 = (bf16[128,16,128]{2,1,0:T(8,128)(2,1)S(1)}, bf16[128,16,128]{2,1,0:T(8,128)(2,1)}, u32[]{:S(2)}) copy-start(bf16[128,16,128]{2,1,0:T(8,128)(2,1)} %d_out.1) | copy-start | bytes 1572868
  28.4 1.0 %copy-start.13 = (bf16[128,16,128]{2,1,0:T(8,128)(2,1)S(1)}, bf16[128,16,128]{2,1,0:T(8,128)(2,1)}, u32[]{:S(2)}) copy-start(bf16[128,16,128]{2,1,0:T(8,128)(2,1)} %attn_out.1) | copy-start | bytes 1572868
  32.7 0.5 copy-start.10
  33.6 0.7 copy-start.11
  33.6 0.7 copy-start.5
  33.6 0.7 copy-start.7
  33.6 0.7 copy-start.9
  50.8 30.7 %collective-permute-start.2 = (bf16[512,128]{1,0:T(8,128)(2,1)S(1)}, bf16[512,128]{1,0:T(8,128)(2,1)S(1)}, u32[]{:S(2)}, u32[]{:S(2)}) collective-permute-start(bf16[512,128]{1,0:T(8,128)(2,1)S(1)} %get-tuple-element.29), channel_id=1, source_target_pairs={{16,0},{32,16},{48,32},{64,48},{80,64},{96,80},{112,96},{128,112},... | collective-permute-start | bytes 393224 | tf_op jit(solution)/shard_map/ppermute | solution.py:251

commit v2 on v1

v2 whole, which is shorter than its diff:
```python
import jax
import jax.numpy as jnp
import numpy as np
from jax import lax
from jax.experimental import pallas as pl
from jax.experimental.pallas import tpu as pltpu
from jax.sharding import PartitionSpec as P

F32 = jnp.float32
BF16 = jnp.bfloat16
EPSILON = 1e-06
TOK = 128
HALF = 64
KV = 2
MEM = 8
DH = 128
ROWS = HALF * MEM
SLOTS = 4
SCALE = DH ** (-0.5)
LOG2E = float(np.log2(np.e))
PAYLOAD = 2 * TOK * KV
EXTRA = 16
STATS = PAYLOAD + 8
FIRST = ("y",)
SECOND = ("zh", "zl", "c")
VMEM = pl.BlockSpec(memory_space=pltpu.VMEM)
SMEM = pl.BlockSpec(memory_space=pltpu.SMEM)
PARAMS = pltpu.CompilerParams(vmem_limit_bytes=12 * 1024 * 1024)


def facts(spans):
    block = (lax.axis_index("zh") * 8 + lax.axis_index("y")) * SLOTS + lax.axis_index("x")
    place = lax.axis_index("x")
    first, second = spans[2 * block], spans[2 * block + 1]
    flip = (first > second).astype(jnp.int32)
    early = jnp.minimum(first, second)
    wraps = [lax.rem(place - slot + SLOTS - 1, SLOTS) + 1 > early for slot in range(SLOTS)]
    return flip, place, wraps


def dot_nt(a, b):
    return lax.dot_general(a, b, (((1,), (1,)), ((), ())), preferred_element_type=F32)


def dot_nn(a, b):
    return lax.dot_general(a, b, (((1,), (0,)), ((), ())), preferred_element_type=F32)


def dot_tn(a, b):
    return lax.dot_general(a, b, (((0,), (0,)), ((), ())), preferred_element_type=F32)


def unit_of(floats):
    inverse = lax.rsqrt(jnp.mean(floats * floats, axis=-1, keepdims=True) + EPSILON)
    return floats * inverse, inverse


def norm_backward(unit, inverse, gain, gradient):
    scaled = gradient * gain
    projected = jnp.mean(scaled * unit, axis=-1, keepdims=True)
    return (scaled - unit * projected) * inverse


def pair(key, value, query, grad_out, lse2, delta, mask=None, keep=None):
    scores = dot_nt(key, query)
    probs = jnp.exp2(scores * (SCALE * LOG2E) - lse2)
    if mask is not None:
        probs = jnp.where(mask, probs, 0.0)
    if keep is not None:
        probs = jnp.concatenate([jnp.where(flag, probs[slot * HALF:(slot + 1) * HALF], 0.0)
                                 for slot, flag in enumerate(keep)], axis=0)
    d_probs = dot_nt(value, grad_out)
    d_scores = (probs * (d_probs - delta)).astype(BF16)
    d_value = dot_nn(probs.astype(BF16), grad_out)
    d_key = dot_nn(d_scores, query) * SCALE
    d_query = dot_tn(d_scores, key) * SCALE
    return d_query, d_key, d_value


def split(scratch, at, group):
    first = scratch[at, pl.ds(group, HALF, stride=KV), :].astype(BF16)
    second = scratch[at, pl.ds(TOK + group, HALF, stride=KV), :].astype(BF16)
    return first, second


def prep_kernel(spans, q_raw, d_out, attn_out, lse2, k_raw, values, q_gain, k_gain,
                q_norm, grads_out, d_query, d_local, keys, made, stats):
    flip, _, wrapped = facts(spans)
    flipped = flip == 1
    gain = q_gain[...].reshape(1, DH)
    ones = jnp.ones((8, DH), F32)
    for group in range(KV):
        q_rows = q_raw[...].astype(F32)[:, group * MEM:(group + 1) * MEM, :]
        unit, _ = unit_of(q_rows.reshape(TOK * MEM, DH))
        normed = (unit * gain).astype(BF16)
        grads = d_out[...].astype(F32)[:, group * MEM:(group + 1) * MEM, :].reshape(TOK * MEM, DH)
        outs = attn_out[...].astype(F32)[:, group * MEM:(group + 1) * MEM, :].reshape(TOK * MEM, DH)
        row_delta = lax.dot_general(ones, grads * outs, (((1,), (1,)), ((), ())),
                                    precision=lax.Precision.HIGHEST, preferred_element_type=F32)
        grads = grads.astype(BF16)
        for half in range(2):
            rows = slice(half * ROWS, (half + 1) * ROWS)
            q_norm[group, half] = normed[rows]
            grads_out[group, half] = grads[rows]
            stats[group, half, 0:1] = lse2[group, half]
            stats[group, half, 1:2] = row_delta[0:1, rows]

    k_unit, _ = unit_of(k_raw[...].astype(F32))
    keys[0] = (k_unit * k_gain[...].reshape(1, DH)).astype(BF16).astype(F32)
    keys[1] = values[...].astype(F32)
    key_at = lax.broadcasted_iota(jnp.int32, (HALF, ROWS), 0)
    query_at = lax.broadcasted_iota(jnp.int32, (HALF, ROWS), 1) // MEM
    mask = key_at <= query_at
    late = 1 - flip
    for group in range(KV):
        key = split(keys, 0, group)
        value = split(keys, 1, group)
        d_key = []
        d_value = []
        for half in range(2):
            dq, dk, dv = pair(key[half], value[half], q_norm[group, half], grads_out[group, half],
                              stats[group, half, 0:1], stats[group, half, 1:2], mask)
            d_query[group, half] = dq
            d_key.append(dk)
            d_value.append(dv)
        early_key = jnp.where(flipped, key[1], key[0])
        early_value = jnp.where(flipped, value[1], value[0])
        dq, dk, dv = pair(early_key, early_value, q_norm[group, late], grads_out[group, late],
                          stats[group, late, 0:1], stats[group, late, 1:2])
        d_query[group, late] += dq
        for half in range(2):
            here = flipped if half == 1 else jnp.logical_not(flipped)
            rows = pl.ds(half * TOK + group, HALF, stride=KV)
            made[0, rows, :] = d_key[half] + jnp.where(here, dk, 0.0)
            made[1, rows, :] = d_value[half] + jnp.where(here, dv, 0.0)
    for group in range(KV):
        for half in range(2):
            base = STATS + (group * 2 + half) * 8
            for part in range(4):
                lanes = slice(part * DH, (part + 1) * DH)
                d_local[base + part:base + part + 1] = stats[group, half, 0:1, lanes]
                d_local[base + 4 + part:base + 5 + part] = stats[group, half, 1:2, lanes]
    d_local[0:TOK * KV] = made[0]
    d_local[TOK * KV:PAYLOAD] = made[1]
    flags = [jnp.full((1, DH), flag, jnp.int32).astype(F32) for flag in [flip] + [w.astype(jnp.int32) for w in wrapped]]
    d_local[PAYLOAD:PAYLOAD + 8] = jnp.concatenate(
        [jnp.sum(made[0] * k_unit, axis=0, keepdims=True), gain, k_gain[...].reshape(1, DH)] + flags, axis=0)


def build_kernel(k_own, v_own, k_behind, v_behind, out):
    place = lax.axis_index("x")
    for slot in range(SLOTS):
        own = slot > place
        out[slot, 0:TOK * KV] = jnp.where(own, k_own[...], k_behind[...])
        out[slot, TOK * KV:PAYLOAD] = jnp.where(own, v_own[...], v_behind[...])


def three_terms(row):
    high = row.astype(BF16).astype(F32)
    rest = row - high
    middle = rest.astype(BF16).astype(F32)
    return [high, middle, rest - middle]


def main_kernel(blocks, q_norm, grads_out, d_query0, q_raw, d_local,
                d_q_raw, pieces, d_query, units, keys, vals, grads, sums):
    q_gain, k_gain = d_local[PAYLOAD + 1:PAYLOAD + 2], d_local[PAYLOAD + 2:PAYLOAD + 3]
    flags = [jnp.max(d_local[PAYLOAD + at:PAYLOAD + at + 1]).astype(jnp.int32) for at in range(3, 8)]
    flip, wrapped = flags[0], [flag == 1 for flag in flags[1:]]
    flipped = flip == 1
    late = 1 - flip
    inside = [jnp.logical_not(flag) for flag in wrapped]
    some_inside = inside[0] | inside[1] | inside[2] | inside[3]
    some_wrapped = wrapped[0] | wrapped[1] | wrapped[2] | wrapped[3]
    for slot in range(SLOTS):
        unit, _ = unit_of(blocks[slot, 0:TOK * KV].astype(F32))
        units[slot] = unit
        keys[slot] = (unit * k_gain).astype(BF16).astype(F32)
        vals[slot] = blocks[slot, TOK * KV:PAYLOAD].astype(F32)

    def stats(group, half):
        rows = d_local[pl.ds(pl.multiple_of(STATS + (group * 2 + half) * 8, 8), 8), :]
        return [jnp.concatenate([rows[at + part:at + part + 1] for part in range(4)], axis=1) for at in (0, 4)]

    d_query[...] = d_query0[...]
    for group in range(KV):
        def gather(scratch, want_late):
            halves = [split(scratch, slot, group) for slot in range(SLOTS)]
            first = flipped if want_late else jnp.logical_not(flipped)
            return jnp.concatenate([jnp.where(first, half[0], half[1]) for half in halves], axis=0)

        early_keys, early_values = gather(keys, False), gather(vals, False)
        dq, dk, dv = pair(early_keys, early_values, q_norm[group, late], grads_out[group, late],
                          *stats(group, late))
        d_query[group, late] += dq
        sums[0] = dk
        sums[1] = dv
        sums[2] = jnp.zeros_like(dk)
        sums[3] = jnp.zeros_like(dv)

        @pl.when(some_inside)
        def _():
            dq, dk, dv = pair(early_keys, early_values, q_norm[group, flip], grads_out[group, flip],
                              *stats(group, flip), keep=inside)
            d_query[group, flip] += dq
            sums[0] += dk
            sums[1] += dv

        @pl.when(some_wrapped)
        def _():
            dq, dk, dv = pair(gather(keys, True), gather(vals, True), q_norm[group, late], grads_out[group, late],
                              *stats(group, late), keep=wrapped)
            d_query[group, late] += dq
            sums[2] = dk
            sums[3] = dv

        for slot in range(SLOTS):
            span = slice(slot * HALF, (slot + 1) * HALF)
            for which in range(2):
                of_early, of_late = sums[which, span], sums[2 + which, span]
                at = slot * 2 + which
                grads[at, pl.ds(group, HALF, stride=KV), :] = jnp.where(flipped, of_late, of_early)
                grads[at, pl.ds(TOK + group, HALF, stride=KV), :] = jnp.where(flipped, of_early, of_late)

    k_sum = d_local[PAYLOAD:PAYLOAD + 1]
    for slot in range(SLOTS):
        k_sum += jnp.sum(grads[2 * slot] * units[slot], axis=0, keepdims=True)
        pieces[slot, 0:TOK * KV] = grads[2 * slot].astype(BF16)
        pieces[slot, TOK * KV:PAYLOAD] = grads[2 * slot + 1].astype(BF16)

    q_sum = jnp.zeros((1, DH), F32)
    gain = q_gain
    for half in range(2):
        tokens = slice(half * HALF, (half + 1) * HALF)
        raw = q_raw[tokens].astype(F32)
        made = []
        for group in range(KV):
            rows = raw[:, group * MEM:(group + 1) * MEM, :].reshape(ROWS, DH)
            unit, inverse = unit_of(rows)
            gradient = d_query[group, half]
            q_sum += jnp.sum(gradient * unit, axis=0, keepdims=True)
            made.append(norm_backward(unit, inverse, gain, gradient).reshape(HALF, MEM, DH))
        d_q_raw[tokens] = jnp.concatenate(made, axis=1).astype(BF16)

    terms = three_terms(q_sum) + three_terms(k_sum) + [jnp.zeros((EXTRA - 6, DH), F32)]
    extra = jnp.concatenate(terms, axis=0).astype(BF16)
    for slot in range(SLOTS):
        pieces[slot, PAYLOAD:PAYLOAD + EXTRA] = extra


def sum_kernel(pieces, d_local, own, behind, gains):
    place = lax.axis_index("x")
    total = d_local[0:PAYLOAD]
    others = jnp.zeros((PAYLOAD, DH), F32)
    extra = jnp.zeros((EXTRA, DH), F32)
    for slot in range(SLOTS):
        piece = pieces[slot, 0:PAYLOAD].astype(F32)
        ahead = slot > place
        total += jnp.where(ahead, piece, 0.0)
        others += jnp.where(ahead, 0.0, piece)
        extra += pieces[slot, PAYLOAD:PAYLOAD + EXTRA].astype(F32)
    own[...] = total
    behind[...] = others.astype(BF16)
    both = jnp.concatenate([jnp.sum(extra[0:3], axis=0, keepdims=True), jnp.sum(extra[3:6], axis=0, keepdims=True)], axis=0)
    for peer in range(gains.shape[0]):
        gains[peer] = both


def relay_kernel(gathered, spread):
    both = jnp.sum(gathered[...], axis=0)
    for peer in range(spread.shape[0]):
        spread[peer] = both


def last_kernel(own, arrived, k_raw, k_gain, gathered, d_k_raw, d_values, q_sum, k_sum):
    total = own[...] + arrived[...].astype(F32)
    unit, inverse = unit_of(k_raw[...].astype(F32))
    d_k_raw[...] = norm_backward(unit, inverse, k_gain[...].reshape(1, DH), total[0:TOK * KV]).astype(BF16)
    d_values[...] = total[TOK * KV:PAYLOAD].astype(BF16)
    both = jnp.sum(gathered[...], axis=0)
    q_sum[...] = both[0]
    k_sum[...] = both[1]


def call(kernel, outs, specs, scratch=(), flops=0, size=0):
    return pl.pallas_call(
        kernel,
        out_shape=[jax.ShapeDtypeStruct(*o) for o in outs],
        in_specs=specs,
        out_specs=[VMEM] * len(outs),
        scratch_shapes=list(scratch),
        compiler_params=PARAMS,
        cost_estimate=pl.CostEstimate(flops=flops, bytes_accessed=size, transcendentals=0),
    )


def step(block, axes, distance):
    size = lax.axis_size(axes)
    return lax.ppermute(block, axes, [((i - distance) % size, i) for i in range(size)])


def per_device(q_raw, k_raw, values, attn_out, d_out, lse, q_gain, k_gain, span_order):
    k_own = k_raw.reshape(TOK * KV, DH)
    v_own = values.reshape(TOK * KV, DH)
    k_behind = step(k_own, ("zh", "y"), 1)
    v_behind = step(v_own, ("zh", "y"), 1)

    lse2 = (lse * LOG2E).reshape(KV, MEM, TOK).transpose(0, 2, 1).reshape(KV, 2, 1, ROWS)

    q_norm, grads_out, d_query0, d_local = call(
        prep_kernel,
        [((KV, 2, ROWS, DH), BF16), ((KV, 2, ROWS, DH), BF16),
         ((KV, 2, ROWS, DH), F32), ((STATS + KV * 2 * 8, DH), F32)],
        [SMEM] + [VMEM] * 8,
        [pltpu.VMEM((2, TOK * KV, DH), F32)] * 2 + [pltpu.VMEM((KV, 2, 8, ROWS), F32)],
        flops=int(6e9), size=1 << 22,
    )(span_order, q_raw, d_out, attn_out, lse2, k_own, v_own, q_gain, k_gain)

    (blocks,) = call(build_kernel, [((SLOTS, PAYLOAD, DH), BF16)], [VMEM] * 4)(
        k_own, v_own, k_behind, v_behind)
    blocks = lax.all_to_all(blocks, "x", 0, 0)
    d_q_raw, pieces = call(
        main_kernel,
        [((TOK, KV * MEM, DH), BF16), ((SLOTS, PAYLOAD + EXTRA, DH), BF16)],
        [VMEM] * 6,
        [pltpu.VMEM((KV, 2, ROWS, DH), F32)] + [pltpu.VMEM((SLOTS, TOK * KV, DH), F32)] * 3
        + [pltpu.VMEM((2 * SLOTS, TOK * KV, DH), F32), pltpu.VMEM((4, SLOTS * HALF, DH), F32)],
    )(blocks, q_norm, grads_out, d_query0, q_raw, d_local)
    pieces = lax.all_to_all(pieces, "x", 0, 0)
    own, behind, gains = call(
        sum_kernel,
        [((PAYLOAD, DH), F32), ((PAYLOAD, DH), BF16), ((lax.axis_size(FIRST), 2, DH), F32)],
        [VMEM] * 2,
    )(pieces, d_local)
    arrived = step(behind, ("zh", "y"), -1)
    gains = lax.all_to_all(gains, FIRST, 0, 0)
    (gains,) = call(relay_kernel, [((lax.axis_size(SECOND), 2, DH), F32)], [VMEM])(gains)
    gains = lax.all_to_all(gains, SECOND, 0, 0)
    d_k_raw, d_values, d_q_gain, d_k_gain = call(
        last_kernel,
        [((TOK * KV, DH), BF16), ((TOK * KV, DH), BF16), ((DH,), F32), ((DH,), F32)],
        [VMEM] * 5,
    )(own, arrived, k_own, k_gain, gains)
    return (d_q_raw, d_k_raw.reshape(TOK, KV, DH), d_values.reshape(TOK, KV, DH),
            d_q_gain, d_k_gain)


def solution(mesh):
    devices = np.asarray(mesh.devices).reshape(4, 8, 4, 2, 2)
    mesh = jax.sharding.Mesh(devices, ("zh", "y", "x", "zl", "c"))
    rows = ("zh", "y", "x")
    heads = ("zl", "c")
    placed = P(rows, heads, None)
    return jax.shard_map(
        per_device,
        mesh=mesh,
        in_specs=(placed,) * 5 + (P(heads, rows), P(), P(), P()),
        out_specs=(placed,) * 3 + (P(), P()),
        check_vma=False,
    )
```

time: 82.9 us -> 78 us (0.941)
  waiting for transfers between devices: 8.7 us -> 12.3 us
  local copies, waits for them, and re-layouts: 6.05 us -> 3.18 us
  between operations: 3.36 us -> 0.72 us
  Pallas kernels: 11.4 us -> 9.56 us
  starting transfers between devices: 15 us -> 13.3 us
    ppermute x3, waiting for transfers between devices: 8.29 us -> 11.6 us  [step(): lax.ppermute(block, axes, [((i - distance) % size, i) for i in range(size)])]
    unnamed x32 -> x18, local copies, waits for them, and re-layouts: 5.16 us -> 2.94 us
    ppermute x3, starting transfers between devices: 10.8 us -> 9.16 us  [step(): lax.ppermute(block, axes, [((i - distance) % size, i) for i in range(size)])]
    pallas_call x1, Pallas kernels: 5.06 us -> 4.2 us  [per_device(): call(main_kernel, [((TOK, KV * MEM, DH), BF16), ((SLOTS, PAYLOAD + EXTRA,...]
where the time goes in v2:
time: 78 us; the launch traced here: 77.4 us
  blocking collectives  37.6 us (48%)
  starting transfers between devices  13.3 us (17%)
  waiting for transfers between devices  12.3 us (16%)
  Pallas kernels  9.56 us (12%)
  local copies, waits for them, and re-layouts  3.18 us (4%)
    all_to_all x1, blocking collectives, per_device(): gains = lax.all_to_all(gains, SECOND, 0, 0)  18.1 us
    ppermute x3, waiting for transfers between devices, step(): lax.ppermute(block, axes, [((i - distance) % size, i) for i in range(size)])  11.6 us
    all_to_all x1, blocking collectives, per_device(): pieces = lax.all_to_all(pieces, 'x', 0, 0)  10.4 us
    ppermute x3, starting transfers between devices, step(): lax.ppermute(block, axes, [((i - distance) % size, i) for i in range(size)])  9.16 us
    all_to_all x1, blocking collectives, per_device(): gains = lax.all_to_all(gains, FIRST, 0, 0)  9.1 us
    pallas_call x1, Pallas kernels, per_device(): call(main_kernel, [((TOK, KV * MEM, DH), BF16), ((SLOTS, PAYLOAD + EXTRA,...  4.2 us
    all_to_all x1, starting transfers between devices, per_device(): blocks = lax.all_to_all(blocks, 'x', 0, 0)  4.16 us
    pallas_call x1, Pallas kernels, per_device(): call(prep_kernel, [((KV, 2, ROWS, DH), BF16), ((KV, 2, ROWS, DH), BF16),...  3.37 us
  transfers between devices with their start and end apart: 4, of which 3 were waited for; matrix products, arithmetic and copies ran while one was open for 1% of the time, Pallas kernels for 4%

profile of v2, /device:TPU:1, one launch (start us, length us, event | category | flops | bytes accessed | tf_op | source)
XLA Modules:
  0.0 77.4 jit_solution(16358452030629779689)
XLA Ops:
  0.6 4.0 %collective-permute-start = (bf16[256,128]{1,0:T(8,128)(2,1)}, bf16[256,128]{1,0:T(8,128)(2,1)S(1)}, u32[]{:S(2)}, u32[]{:S(2)}) collective-permute-start(bf16[256,128]{1,0:T(8,128)(2,1)} %bitcast.7), channel_id=1, source_target_pairs={{496,0},{0,16},{16,32},{32,48},{48,64},{64,80},{80,96},{96,112},{1... | collective-permute-start | bytes 196616 | tf_op jit(solution)/shard_map/ppermute | solution.py:299
  4.7 3.2 %collective-permute-start.1 = (bf16[256,128]{1,0:T(8,128)(2,1)}, bf16[256,128]{1,0:T(8,128)(2,1)S(1)}, u32[]{:S(2)}, u32[]{:S(2)}) collective-permute-start(bf16[256,128]{1,0:T(8,128)(2,1)} %bitcast.11), channel_id=1, source_target_pairs={{496,0},{0,16},{16,32},{32,48},{48,64},{64,80},{80,96},{96,112},{1... | collective-permute-start | bytes 196616 | tf_op jit(solution)/shard_map/ppermute | solution.py:299
  7.9 0.7 multiply_bitcast_fusion
  8.6 0.1 copy.15
  8.7 0.0 copy-start.1
  8.7 0.0 copy-start.2
  8.7 0.1 reshape.34.lse2
  8.9 8.7 %collective-permute-done.k_behind = bf16[256,128]{1,0:T(8,128)(2,1)S(1)} collective-permute-done((bf16[256,128]{1,0:T(8,128)(2,1)}, bf16[256,128]{1,0:T(8,128)(2,1)S(1)}, u32[]{:S(2)}, u32[]{:S(2)}) %collective-permute-start) | collective-permute-done | bytes 65568 | tf_op jit(solution)/shard_map/ppermute | solution.py:299
  17.6 2.9 %collective-permute-done.1.v_behind = bf16[256,128]{1,0:T(8,128)(2,1)S(1)} collective-permute-done((bf16[256,128]{1,0:T(8,128)(2,1)}, bf16[256,128]{1,0:T(8,128)(2,1)S(1)}, u32[]{:S(2)}, u32[]{:S(2)}) %collective-permute-start.1) | collective-permute-done | bytes 65568 | tf_op jit(solution)/shard_map/ppermute | solution.py:299
  20.5 0.0 copy-done.1
  20.5 0.0 copy-done.2
  20.5 0.9 %shard_map.128 = bf16[4,512,128]{2,1,0:T(8,128)(2,1)} custom-call(bf16[256,128]{1,0:T(8,128)(2,1)S(1)} %bitcast.8, bf16[256,128]{1,0:T(8,128)(2,1)S(1)} %bitcast.12, bf16[256,128]{1,0:T(8,128)(2,1)S(1)} %collective-permute-done.k_behind, bf16[256,128]{1,0:T(8,128)(2,1)S(1)} %collective-permute-done.1.v_behind), custom_call_target="tpu_custom_call" | custom-call | tf_op jit(solution)/shard_map/pallas_call | solution.py:319
  21.4 0.0 copy-start
  21.4 4.2 %all-to-all-start = ((bf16[4,512,128]{2,1,0:T(8,128)(2,1)}), bf16[4,512,128]{2,1,0:T(8,128)(2,1)S(1)}, u32[]{:S(2)}, u32[]{:S(2)}) async-start(bf16[4,512,128]{2,1,0:T(8,128)(2,1)} %shard_map.128), calls=%async_computation | async-start | bytes 1048576 | tf_op jit(solution)/shard_map/all_to_all | solution.py:321
  25.6 0.0 copy-done
  25.6 0.0 copy-done.4
  25.6 0.0 copy-done.7
  25.6 0.0 copy-done.8
  25.6 0.0 copy-start.3
  25.6 0.8 %copy-done.3 = bf16[128,2,128]{2,1,0:T(2,128)(2,1)S(1)} copy-done((bf16[128,2,128]{2,1,0:T(2,128)(2,1)S(1)}, bf16[128,2,128]{2,1,0:T(2,128)(2,1)}, u32[]{:S(2)}) %copy-start.3) | copy-done | bytes 65560
  26.5 1.0 %copy-done.5 = bf16[128,16,128]{2,1,0:T(8,128)(2,1)S(1)} copy-done((bf16[128,16,128]{2,1,0:T(8,128)(2,1)S(1)}, bf16[128,16,128]{2,1,0:T(8,128)(2,1)}, u32[]{:S(2)}) %copy-start.5) | copy-done | bytes 524312
  27.5 1.0 %copy-done.6 = bf16[128,16,128]{2,1,0:T(8,128)(2,1)S(1)} copy-done((bf16[128,16,128]{2,1,0:T(8,128)(2,1)S(1)}, bf16[128,16,128]{2,1,0:T(8,128)(2,1)}, u32[]{:S(2)}) %copy-start.6) | copy-done | bytes 524312
  28.6 3.4 %shard_map.129 = (bf16[2,2,512,128]{3,2,1,0:T(8,128)(2,1)S(1)}, bf16[2,2,512,128]{3,2,1,0:T(8,128)(2,1)S(1)}, f32[2,2,512,128]{3,2,1,0:T(8,128)S(1)}, f32[552,128]{1,0:T(8,128)S(1)}) custom-call(s32[256]{0:T(256)S(1)} %copy-done.7, bf16[128,16,128]{2,1,0:T(8,128)(2,1)S(1)} %copy-done, bf16[128,16,128]{2,1,0:T(8,128)(2,1)S(1)} %copy-done.5, ...), custom_call_target="tpu_custom_call" | custom-call | flops 6000000000 | bytes 4194304 | tf_op jit(solution)/shard_map/pallas_call | solution.py:310
  31.9 0.7 all-to-all-done.blocks
  32.6 4.2 %shard_map.130 = (bf16[128,16,128]{2,1,0:T(8,128)(2,1)}, bf16[4,528,128]{2,1,0:T(8,128)(2,1)S(1)}) custom-call(bf16[4,512,128]{2,1,0:T(8,128)(2,1)S(1)} %all-to-all-done.blocks, bf16[2,2,512,128]{3,2,1,0:T(8,128)(2,1)S(1)} %get-tuple-element.18.q_norm, bf16[2,2,512,128]{3,2,1,0:T(8,128)(2,1)S(1)} %get-tuple-element.19.grads_out, ...), custom_call_target="tpu_custom_call" | custom-call | tf_op jit(solution)/shard_map/pallas_call | solution.py:322
  36.8 10.4 %all_to_all.20.pieces = bf16[4,528,128]{2,1,0:T(8,128)(2,1)S(1)} all-to-all(bf16[4,528,128]{2,1,0:T(8,128)(2,1)S(1)} %get-tuple-element.23), channel_id=1, replica_groups=mesh['zh'=4,'y'=8,'x'=4,'zl'=2,'c'=2] {'x'}, dimensions={0} | all-to-all | bytes 1081344 | tf_op jit(solution)/shard_map/all_to_all | solution.py:329
  47.2 0.2 shard_map.131
  47.4 1.9 %collective-permute-start.2 = (bf16[512,128]{1,0:T(8,128)(2,1)S(1)}, bf16[512,128]{1,0:T(8,128)(2,1)S(1)}, u32[]{:S(2)}, u32[]{:S(2)}) collective-permute-start(bf16[512,128]{1,0:T(8,128)(2,1)S(1)} %get-tuple-element.25), channel_id=1, source_target_pairs={{16,0},{32,16},{48,32},{64,48},{80,64},{96,80},{112,96},{128,112},... | collective-permute-start | bytes 393224 | tf_op jit(solution)/shard_map/ppermute | solution.py:299
  49.3 9.1 %all_to_all.21.gathered = f32[8,2,128]{2,1,0:T(2,128)S(1)} all-to-all(f32[8,2,128]{2,1,0:T(2,128)S(1)} %get-tuple-element.26), channel_id=1, replica_groups=mesh['zh'=4,'y'=8,'x'=4,'zl'=2,'c'=2] {'y'}, dimensions={0} | all-to-all | bytes 16384 | tf_op jit(solution)/shard_map/all_to_all | solution.py:336
  58.4 18.1 %all_to_all.22.gathered = f32[16,2,128]{2,1,0:T(2,128)S(1)} all-to-all(f32[16,2,128]{2,1,0:T(2,128)S(1)} %shard_map.132), channel_id=1, replica_groups=mesh['zh'=4,'y'=8,'x'=4,'zl'=2,'c'=2] {'zh','zl','c'}, dimensions={0} | all-to-all | bytes 32768 | tf_op jit(solution)/shard_map/all_to_all | solution.py:338
  76.6 0.0 collective-permute-done.2.arrived
  76.6 0.8 %shard_map.133 = (bf16[256,128]{1,0:T(8,128)(2,1)}, bf16[256,128]{1,0:T(8,128)(2,1)}, f32[128]{0:T(128)}, f32[128]{0:T(128)}) custom-call(f32[512,128]{1,0:T(8,128)S(1)} %get-tuple-element.24.own, bf16[512,128]{1,0:T(8,128)(2,1)S(1)} %collective-permute-done.2.arrived, bf16[256,128]{1,0:T(8,128)(2,1)S(1)} %bitcast.10, f32[128]{0:T(128)S(1)} %copy-done.4, ...), custom_call_target="tpu_custom_call" | custom-call | tf_op jit(solution)/shard_map/pallas_call | solution.py:339
  (6 shorter events, 0.0 us)
Async XLA Ops:
  0.6 16.9 %collective-permute-start = (bf16[256,128]{1,0:T(8,128)(2,1)}, bf16[256,128]{1,0:T(8,128)(2,1)S(1)}, u32[]{:S(2)}, u32[]{:S(2)}) collective-permute-start(bf16[256,128]{1,0:T(8,128)(2,1)} %bitcast.7), channel_id=1, source_target_pairs={{496,0},{0,16},{16,32},{32,48},{48,64},{64,80},{80,96},{96,112},{1... | collective-permute-start | bytes 196616 | tf_op jit(solution)/shard_map/ppermute | solution.py:299
  4.7 15.8 %collective-permute-start.1 = (bf16[256,128]{1,0:T(8,128)(2,1)}, bf16[256,128]{1,0:T(8,128)(2,1)S(1)}, u32[]{:S(2)}, u32[]{:S(2)}) collective-permute-start(bf16[256,128]{1,0:T(8,128)(2,1)} %bitcast.11), channel_id=1, source_target_pairs={{496,0},{0,16},{16,32},{32,48},{48,64},{64,80},{80,96},{96,112},{1... | collective-permute-start | bytes 196616 | tf_op jit(solution)/shard_map/ppermute | solution.py:299
  8.7 11.8 %copy-start.1 = (bf16[128,2,128]{2,1,0:T(2,128)(2,1)S(1)}, bf16[128,2,128]{2,1,0:T(2,128)(2,1)}, u32[]{:S(2)}) copy-start(bf16[128,2,128]{2,1,0:T(2,128)(2,1)} %param.10) | copy-start | bytes 196612
  8.7 11.8 %copy-start.2 = (bf16[128,2,128]{2,1,0:T(2,128)(2,1)S(1)}, bf16[128,2,128]{2,1,0:T(2,128)(2,1)}, u32[]{:S(2)}) copy-start(bf16[128,2,128]{2,1,0:T(2,128)(2,1)} %param.11) | copy-start | bytes 196612
  21.4 4.2 %copy-start = (bf16[128,16,128]{2,1,0:T(8,128)(2,1)S(1)}, bf16[128,16,128]{2,1,0:T(8,128)(2,1)}, u32[]{:S(2)}) copy-start(bf16[128,16,128]{2,1,0:T(8,128)(2,1)} %q_raw.3) | copy-start | bytes 1572868
  21.4 4.2 %copy-start.4 = (f32[128]{0:T(128)S(1)}, f32[128]{0:T(128)}, u32[]{:S(2)}) copy-start(f32[128]{0:T(128)} %k_gain.3) | copy-start | bytes 1540
  21.4 4.2 %copy-start.7 = (s32[256]{0:T(256)S(1)}, s32[256]{0:T(256)}, u32[]{:S(2)}) copy-start(s32[256]{0:T(256)} %spans.1) | copy-start | bytes 3076
  21.4 4.2 %copy-start.8 = (f32[128]{0:T(128)S(1)}, f32[128]{0:T(128)}, u32[]{:S(2)}) copy-start(f32[128]{0:T(128)} %q_gain.1) | copy-start | bytes 1540
  21.4 11.1 %all-to-all-start = ((bf16[4,512,128]{2,1,0:T(8,128)(2,1)}), bf16[4,512,128]{2,1,0:T(8,128)(2,1)S(1)}, u32[]{:S(2)}, u32[]{:S(2)}) async-start(bf16[4,512,128]{2,1,0:T(8,128)(2,1)} %shard_map.128), calls=%async_computation | async-start | bytes 1048576 | tf_op jit(solution)/shard_map/all_to_all | solution.py:321
  25.6 0.8 %copy-start.3 = (bf16[128,2,128]{2,1,0:T(2,128)(2,1)S(1)}, bf16[128,2,128]{2,1,0:T(2,128)(2,1)}, u32[]{:S(2)}) copy-start(bf16[128,2,128]{2,1,0:T(2,128)(2,1)} %param.11) | copy-start | bytes 196612
  26.5 1.0 %copy-start.5 = (bf16[128,16,128]{2,1,0:T(8,128)(2,1)S(1)}, bf16[128,16,128]{2,1,0:T(8,128)(2,1)}, u32[]{:S(2)}) copy-start(bf16[128,16,128]{2,1,0:T(8,128)(2,1)} %d_out.1) | copy-start | bytes 1572868
  27.5 1.0 %copy-start.6 = (bf16[128,16,128]{2,1,0:T(8,128)(2,1)S(1)}, bf16[128,16,128]{2,1,0:T(8,128)(2,1)}, u32[]{:S(2)}) copy-start(bf16[128,16,128]{2,1,0:T(8,128)(2,1)} %attn_out.1) | copy-start | bytes 1572868
  47.4 29.2 %collective-permute-start.2 = (bf16[512,128]{1,0:T(8,128)(2,1)S(1)}, bf16[512,128]{1,0:T(8,128)(2,1)S(1)}, u32[]{:S(2)}, u32[]{:S(2)}) collective-permute-start(bf16[512,128]{1,0:T(8,128)(2,1)S(1)} %get-tuple-element.25), channel_id=1, source_target_pairs={{16,0},{32,16},{48,32},{64,48},{80,64},{96,80},{112,96},{128,112},... | collective-permute-start | bytes 393224 | tf_op jit(solution)/shard_map/ppermute | solution.py:299

commit v3 on v2

--- a/solution.py
+++ b/solution.py
@@ -20,9 +20,11 @@
 LOG2E = float(np.log2(np.e))
 PAYLOAD = 2 * TOK * KV
 EXTRA = 16
+BUILD_SIZE = 1 << 20
 STATS = PAYLOAD + 8
-FIRST = ("y",)
-SECOND = ("zh", "zl", "c")
+FIRST = ("zh", "zl", "c")
+SECOND = ("y",)
+ANY = pl.BlockSpec(memory_space=pl.ANY)
 VMEM = pl.BlockSpec(memory_space=pltpu.VMEM)
 SMEM = pl.BlockSpec(memory_space=pltpu.SMEM)
 PARAMS = pltpu.CompilerParams(vmem_limit_bytes=12 * 1024 * 1024)
@@ -147,12 +149,24 @@
         [jnp.sum(made[0] * k_unit, axis=0, keepdims=True), gain, k_gain[...].reshape(1, DH)] + flags, axis=0)
 
 
-def build_kernel(k_own, v_own, k_behind, v_behind, out):
+def build_kernel(k_own, v_own, k_behind, v_behind, out, sems):
     place = lax.axis_index("x")
     for slot in range(SLOTS):
-        own = slot > place
-        out[slot, 0:TOK * KV] = jnp.where(own, k_own[...], k_behind[...])
-        out[slot, TOK * KV:PAYLOAD] = jnp.where(own, v_own[...], v_behind[...])
+        for which, (own, behind) in enumerate(((k_own, k_behind), (v_own, v_behind))):
+            target = out.at[slot, pl.ds(which * TOK * KV, TOK * KV)]
+
+            @pl.when(slot > place)
+            def _():
+                pltpu.make_async_copy(own, target, sems.at[slot, which]).start()
+
+            @pl.when(slot <= place)
+            def _():
+                pltpu.make_async_copy(behind, target, sems.at[slot, which]).start()
+
+    for slot in range(SLOTS):
+        for which in range(2):
+            target = out.at[slot, pl.ds(which * TOK * KV, TOK * KV)]
+            pltpu.make_async_copy(k_behind, target, sems.at[slot, which]).wait()
 
 
 def three_terms(row):
@@ -163,7 +177,7 @@
 
 
 def main_kernel(blocks, q_norm, grads_out, d_query0, q_raw, d_local,
-                d_q_raw, pieces, d_query, units, keys, vals, grads, sums):
+                d_q_raw, pieces, d_query, units, keys, vals, grads, sums, d_q_rows, sems):
     q_gain, k_gain = d_local[PAYLOAD + 1:PAYLOAD + 2], d_local[PAYLOAD + 2:PAYLOAD + 3]
     flags = [jnp.max(d_local[PAYLOAD + at:PAYLOAD + at + 1]).astype(jnp.int32) for at in range(3, 8)]
     flip, wrapped = flags[0], [flag == 1 for flag in flags[1:]]
@@ -182,42 +196,66 @@
         rows = d_local[pl.ds(pl.multiple_of(STATS + (group * 2 + half) * 8, 8), 8), :]
         return [jnp.concatenate([rows[at + part:at + part + 1] for part in range(4)], axis=1) for at in (0, 4)]
 
-    d_query[...] = d_query0[...]
-    for group in range(KV):
-        def gather(scratch, want_late):
-            halves = [split(scratch, slot, group) for slot in range(SLOTS)]
-            first = flipped if want_late else jnp.logical_not(flipped)
-            return jnp.concatenate([jnp.where(first, half[0], half[1]) for half in halves], axis=0)
-
-        early_keys, early_values = gather(keys, False), gather(vals, False)
-        dq, dk, dv = pair(early_keys, early_values, q_norm[group, late], grads_out[group, late],
-                          *stats(group, late))
-        d_query[group, late] += dq
-        sums[0] = dk
-        sums[1] = dv
-        sums[2] = jnp.zeros_like(dk)
-        sums[3] = jnp.zeros_like(dv)
+    early_keys, early_values = [], []
+
+    def gather(scratch, group, want_late):
+        halves = [split(scratch, slot, group) for slot in range(SLOTS)]
+        first = flipped if want_late else jnp.logical_not(flipped)
+        return jnp.concatenate([jnp.where(first, half[0], half[1]) for half in halves], axis=0)
+
+    def finish(half, q_sum):
+        raw = q_raw[pl.ds(pl.multiple_of(half * HALF, HALF), HALF)].astype(F32)
+        made = []
+        for group in range(KV):
+            unit, inverse = unit_of(raw[:, group * MEM:(group + 1) * MEM, :].reshape(ROWS, DH))
+            gradient = d_query[group, half]
+            q_sum += jnp.sum(gradient * unit, axis=0, keepdims=True)
+            made.append(norm_backward(unit, inverse, q_gain, gradient).reshape(HALF, MEM, DH))
+        tokens = pl.ds(pl.multiple_of(half * HALF, HALF), HALF)
+        d_q_rows[tokens] = jnp.concatenate(made, axis=1).astype(BF16)
+        return q_sum, tokens
+
+    for group in range(KV):
+        early_keys.append(gather(keys, group, False))
+        early_values.append(gather(vals, group, False))
+        d_query[group, flip] = d_query0[group, flip]
+        for at in range(4):
+            sums[group, at] = jnp.zeros((SLOTS * HALF, DH), F32)
 
         @pl.when(some_inside)
         def _():
-            dq, dk, dv = pair(early_keys, early_values, q_norm[group, flip], grads_out[group, flip],
+            dq, dk, dv = pair(early_keys[group], early_values[group], q_norm[group, flip], grads_out[group, flip],
                               *stats(group, flip), keep=inside)
             d_query[group, flip] += dq
-            sums[0] += dk
-            sums[1] += dv
+            sums[group, 0] = dk
+            sums[group, 1] = dv
+
+    q_sum, tokens = finish(flip, jnp.zeros((1, DH), F32))
+    early_copy = pltpu.make_async_copy(d_q_rows.at[tokens], d_q_raw.at[tokens], sems.at[0])
+    early_copy.start()
+    for group in range(KV):
+        dq, dk, dv = pair(early_keys[group], early_values[group], q_norm[group, late], grads_out[group, late],
+                          *stats(group, late))
+        d_query[group, late] = d_query0[group, late] + dq
+        sums[group, 0] += dk
+        sums[group, 1] += dv
 
         @pl.when(some_wrapped)
         def _():
-            dq, dk, dv = pair(gather(keys, True), gather(vals, True), q_norm[group, late], grads_out[group, late],
-                              *stats(group, late), keep=wrapped)
+            dq, dk, dv = pair(gather(keys, group, True), gather(vals, group, True), q_norm[group, late],
+                              grads_out[group, late], *stats(group, late), keep=wrapped)
             d_query[group, late] += dq
-            sums[2] = dk
-            sums[3] = dv
-
+            sums[group, 2] = dk
+            sums[group, 3] = dv
+
+    q_sum, tokens = finish(late, q_sum)
+    late_copy = pltpu.make_async_copy(d_q_rows.at[tokens], d_q_raw.at[tokens], sems.at[1])
+    late_copy.start()
+    for group in range(KV):
         for slot in range(SLOTS):
             span = slice(slot * HALF, (slot + 1) * HALF)
             for which in range(2):
-                of_early, of_late = sums[which, span], sums[2 + which, span]
+                of_early, of_late = sums[group, which, span], sums[group, 2 + which, span]
                 at = slot * 2 + which
                 grads[at, pl.ds(group, HALF, stride=KV), :] = jnp.where(flipped, of_late, of_early)
                 grads[at, pl.ds(TOK + group, HALF, stride=KV), :] = jnp.where(flipped, of_early, of_late)
@@ -228,24 +266,12 @@
         pieces[slot, 0:TOK * KV] = grads[2 * slot].astype(BF16)
         pieces[slot, TOK * KV:PAYLOAD] = grads[2 * slot + 1].astype(BF16)
 
-    q_sum = jnp.zeros((1, DH), F32)
-    gain = q_gain
-    for half in range(2):
-        tokens = slice(half * HALF, (half + 1) * HALF)
-        raw = q_raw[tokens].astype(F32)
-        made = []
-        for group in range(KV):
-            rows = raw[:, group * MEM:(group + 1) * MEM, :].reshape(ROWS, DH)
-            unit, inverse = unit_of(rows)
-            gradient = d_query[group, half]
-            q_sum += jnp.sum(gradient * unit, axis=0, keepdims=True)
-            made.append(norm_backward(unit, inverse, gain, gradient).reshape(HALF, MEM, DH))
-        d_q_raw[tokens] = jnp.concatenate(made, axis=1).astype(BF16)
-
     terms = three_terms(q_sum) + three_terms(k_sum) + [jnp.zeros((EXTRA - 6, DH), F32)]
     extra = jnp.concatenate(terms, axis=0).astype(BF16)
     for slot in range(SLOTS):
         pieces[slot, PAYLOAD:PAYLOAD + EXTRA] = extra
+    early_copy.wait()
+    late_copy.wait()
 
 
 def sum_kernel(pieces, d_local, own, behind, gains):
@@ -282,12 +308,12 @@
     k_sum[...] = both[1]
 
 
-def call(kernel, outs, specs, scratch=(), flops=0, size=0):
+def call(kernel, outs, specs, scratch=(), flops=0, size=0, out_specs=None):
     return pl.pallas_call(
         kernel,
         out_shape=[jax.ShapeDtypeStruct(*o) for o in outs],
         in_specs=specs,
-        out_specs=[VMEM] * len(outs),
+        out_specs=out_specs or [VMEM] * len(outs),
         scratch_shapes=list(scratch),
         compiler_params=PARAMS,
         cost_estimate=pl.CostEstimate(flops=flops, bytes_accessed=size, transcendentals=0),
@@ -316,15 +342,17 @@
         flops=int(6e9), size=1 << 22,
     )(span_order, q_raw, d_out, attn_out, lse2, k_own, v_own, q_gain, k_gain)
 
-    (blocks,) = call(build_kernel, [((SLOTS, PAYLOAD, DH), BF16)], [VMEM] * 4)(
-        k_own, v_own, k_behind, v_behind)
+    (blocks,) = call(build_kernel, [((SLOTS, PAYLOAD, DH), BF16)], [VMEM] * 4, [pltpu.SemaphoreType.DMA((SLOTS, 2))],
+                     size=BUILD_SIZE, out_specs=[ANY])(k_own, v_own, k_behind, v_behind)
     blocks = lax.all_to_all(blocks, "x", 0, 0)
     d_q_raw, pieces = call(
         main_kernel,
         [((TOK, KV * MEM, DH), BF16), ((SLOTS, PAYLOAD + EXTRA, DH), BF16)],
         [VMEM] * 6,
         [pltpu.VMEM((KV, 2, ROWS, DH), F32)] + [pltpu.VMEM((SLOTS, TOK * KV, DH), F32)] * 3
-        + [pltpu.VMEM((2 * SLOTS, TOK * KV, DH), F32), pltpu.VMEM((4, SLOTS * HALF, DH), F32)],
+        + [pltpu.VMEM((2 * SLOTS, TOK * KV, DH), F32), pltpu.VMEM((KV, 4, SLOTS * HALF, DH), F32),
+           pltpu.VMEM((TOK, KV * MEM, DH), BF16), pltpu.SemaphoreType.DMA((2,))],
+        out_specs=[ANY, VMEM],
     )(blocks, q_norm, grads_out, d_query0, q_raw, d_local)
     pieces = lax.all_to_all(pieces, "x", 0, 0)
     own, behind, gains = call(

time: 78 us -> 76.4 us (0.979)
  blocking collectives: 37.6 us -> 36.2 us
    all_to_all x1, blocking collectives: 18.1 us -> 9.95 us  [per_device(): gains = lax.all_to_all(gains, SECOND, 0, 0)]
    all_to_all x1, blocking collectives: 9.1 us -> 15.8 us  [per_device(): gains = lax.all_to_all(gains, FIRST, 0, 0)]
where the time goes in v3:
time: 76.4 us; the launch traced here: 75.8 us
  blocking collectives  36.2 us (47%)
  starting transfers between devices  13.3 us (17%)
  waiting for transfers between devices  12.3 us (16%)
  Pallas kernels  9.34 us (12%)
  local copies, waits for them, and re-layouts  3.19 us (4%)
    all_to_all x1, blocking collectives, per_device(): gains = lax.all_to_all(gains, FIRST, 0, 0)  15.8 us
    ppermute x3, waiting for transfers between devices, step(): lax.ppermute(block, axes, [((i - distance) % size, i) for i in range(size)])  11.6 us
    all_to_all x1, blocking collectives, per_device(): pieces = lax.all_to_all(pieces, 'x', 0, 0)  10.4 us
    all_to_all x1, blocking collectives, per_device(): gains = lax.all_to_all(gains, SECOND, 0, 0)  9.95 us
    ppermute x3, starting transfers between devices, step(): lax.ppermute(block, axes, [((i - distance) % size, i) for i in range(size)])  9.16 us
    all_to_all x1, starting transfers between devices, per_device(): blocks = lax.all_to_all(blocks, 'x', 0, 0)  4.16 us
    pallas_call x1, Pallas kernels, per_device(): call(main_kernel, [((TOK, KV * MEM, DH), BF16), ((SLOTS, PAYLOAD + EXTRA,...  4.04 us
    pallas_call x1, Pallas kernels, per_device(): call(prep_kernel, [((KV, 2, ROWS, DH), BF16), ((KV, 2, ROWS, DH), BF16),...  3.37 us
  transfers between devices with their start and end apart: 4, of which 3 were waited for; matrix products, arithmetic and copies ran while one was open for 1% of the time, Pallas kernels for 4%

profile of v3, /device:TPU:1, one launch (start us, length us, event | category | flops | bytes accessed | tf_op | source)
XLA Modules:
  0.0 75.8 jit_solution(5847649147288823490)
XLA Ops:
  0.6 4.0 %collective-permute-start = (bf16[256,128]{1,0:T(8,128)(2,1)}, bf16[256,128]{1,0:T(8,128)(2,1)S(1)}, u32[]{:S(2)}, u32[]{:S(2)}) collective-permute-start(bf16[256,128]{1,0:T(8,128)(2,1)} %bitcast.7), channel_id=1, source_target_pairs={{496,0},{0,16},{16,32},{32,48},{48,64},{64,80},{80,96},{96,112},{1... | collective-permute-start | bytes 196616 | tf_op jit(solution)/shard_map/ppermute | solution.py:325
  4.7 3.2 %collective-permute-start.1 = (bf16[256,128]{1,0:T(8,128)(2,1)}, bf16[256,128]{1,0:T(8,128)(2,1)S(1)}, u32[]{:S(2)}, u32[]{:S(2)}) collective-permute-start(bf16[256,128]{1,0:T(8,128)(2,1)} %bitcast.11), channel_id=1, source_target_pairs={{496,0},{0,16},{16,32},{32,48},{48,64},{64,80},{80,96},{96,112},{1... | collective-permute-start | bytes 196616 | tf_op jit(solution)/shard_map/ppermute | solution.py:325
  7.9 0.7 multiply_bitcast_fusion
  8.6 0.1 copy.15
  8.7 0.0 copy-start.1
  8.7 0.0 copy-start.2
  8.7 0.1 reshape.34.lse2
  8.9 8.7 %collective-permute-done.k_behind = bf16[256,128]{1,0:T(8,128)(2,1)S(1)} collective-permute-done((bf16[256,128]{1,0:T(8,128)(2,1)}, bf16[256,128]{1,0:T(8,128)(2,1)S(1)}, u32[]{:S(2)}, u32[]{:S(2)}) %collective-permute-start) | collective-permute-done | bytes 65568 | tf_op jit(solution)/shard_map/ppermute | solution.py:325
  17.6 2.9 %collective-permute-done.1.v_behind = bf16[256,128]{1,0:T(8,128)(2,1)S(1)} collective-permute-done((bf16[256,128]{1,0:T(8,128)(2,1)}, bf16[256,128]{1,0:T(8,128)(2,1)S(1)}, u32[]{:S(2)}, u32[]{:S(2)}) %collective-permute-start.1) | collective-permute-done | bytes 65568 | tf_op jit(solution)/shard_map/ppermute | solution.py:325
  20.5 0.0 copy-done.1
  20.5 0.0 copy-done.2
  20.5 0.8 %shard_map.128 = bf16[4,512,128]{2,1,0:T(8,128)(2,1)} custom-call(bf16[256,128]{1,0:T(8,128)(2,1)S(1)} %bitcast.8, bf16[256,128]{1,0:T(8,128)(2,1)S(1)} %bitcast.12, bf16[256,128]{1,0:T(8,128)(2,1)S(1)} %collective-permute-done.k_behind, bf16[256,128]{1,0:T(8,128)(2,1)S(1)} %collective-permute-done.1.v_behind), custom_call_target="tpu_custom_call" | custom-call | bytes 1048576 | tf_op jit(solution)/shard_map/pallas_call | solution.py:345
  21.4 0.0 copy-start
  21.4 0.0 copy-start.4
  21.4 0.0 copy-start.7
  21.4 0.0 copy-start.8
  21.4 4.2 %all-to-all-start = ((bf16[4,512,128]{2,1,0:T(8,128)(2,1)}), bf16[4,512,128]{2,1,0:T(8,128)(2,1)S(1)}, u32[]{:S(2)}, u32[]{:S(2)}) async-start(bf16[4,512,128]{2,1,0:T(8,128)(2,1)} %shard_map.128), calls=%async_computation | async-start | bytes 1048576 | tf_op jit(solution)/shard_map/all_to_all | solution.py:347
  25.6 0.0 copy-done.8
  25.6 0.0 copy-start.3
  25.6 0.8 %copy-done.3 = bf16[128,2,128]{2,1,0:T(2,128)(2,1)S(1)} copy-done((bf16[128,2,128]{2,1,0:T(2,128)(2,1)S(1)}, bf16[128,2,128]{2,1,0:T(2,128)(2,1)}, u32[]{:S(2)}) %copy-start.3) | copy-done | bytes 65560
  26.4 1.0 %copy-done.5 = bf16[128,16,128]{2,1,0:T(8,128)(2,1)S(1)} copy-done((bf16[128,16,128]{2,1,0:T(8,128)(2,1)S(1)}, bf16[128,16,128]{2,1,0:T(8,128)(2,1)}, u32[]{:S(2)}) %copy-start.5) | copy-done | bytes 524312
  27.5 1.0 %copy-done.6 = bf16[128,16,128]{2,1,0:T(8,128)(2,1)S(1)} copy-done((bf16[128,16,128]{2,1,0:T(8,128)(2,1)S(1)}, bf16[128,16,128]{2,1,0:T(8,128)(2,1)}, u32[]{:S(2)}) %copy-start.6) | copy-done | bytes 524312
  28.5 3.4 %shard_map.129 = (bf16[2,2,512,128]{3,2,1,0:T(8,128)(2,1)S(1)}, bf16[2,2,512,128]{3,2,1,0:T(8,128)(2,1)S(1)}, f32[2,2,512,128]{3,2,1,0:T(8,128)S(1)}, f32[552,128]{1,0:T(8,128)S(1)}) custom-call(s32[256]{0:T(256)S(1)} %copy-done.7, bf16[128,16,128]{2,1,0:T(8,128)(2,1)S(1)} %copy-done, bf16[128,16,128]{2,1,0:T(8,128)(2,1)S(1)} %copy-done.5, ...), custom_call_target="tpu_custom_call" | custom-call | flops 6000000000 | bytes 4194304 | tf_op jit(solution)/shard_map/pallas_call | solution.py:336
  31.9 0.7 all-to-all-done.blocks
  32.5 4.0 %shard_map.130 = (bf16[128,16,128]{2,1,0:T(8,128)(2,1)}, bf16[4,528,128]{2,1,0:T(8,128)(2,1)S(1)}) custom-call(bf16[4,512,128]{2,1,0:T(8,128)(2,1)S(1)} %all-to-all-done.blocks, bf16[2,2,512,128]{3,2,1,0:T(8,128)(2,1)S(1)} %get-tuple-element.18.q_norm, bf16[2,2,512,128]{3,2,1,0:T(8,128)(2,1)S(1)} %get-tuple-element.19.grads_out, ...), custom_call_target="tpu_custom_call" | custom-call | tf_op jit(solution)/shard_map/pallas_call | solution.py:348
  36.6 10.4 %all_to_all.20.pieces = bf16[4,528,128]{2,1,0:T(8,128)(2,1)S(1)} all-to-all(bf16[4,528,128]{2,1,0:T(8,128)(2,1)S(1)} %get-tuple-element.23), channel_id=1, replica_groups=mesh['zh'=4,'y'=8,'x'=4,'zl'=2,'c'=2] {'x'}, dimensions={0} | all-to-all | bytes 1081344 | tf_op jit(solution)/shard_map/all_to_all | solution.py:357
  47.0 0.2 shard_map.131
  47.2 1.9 %collective-permute-start.2 = (bf16[512,128]{1,0:T(8,128)(2,1)S(1)}, bf16[512,128]{1,0:T(8,128)(2,1)S(1)}, u32[]{:S(2)}, u32[]{:S(2)}) collective-permute-start(bf16[512,128]{1,0:T(8,128)(2,1)S(1)} %get-tuple-element.25), channel_id=1, source_target_pairs={{16,0},{32,16},{48,32},{64,48},{80,64},{96,80},{112,96},{128,112},... | collective-permute-start | bytes 393224 | tf_op jit(solution)/shard_map/ppermute | solution.py:325
  49.2 15.8 %all_to_all.21.gathered = f32[16,2,128]{2,1,0:T(2,128)S(1)} all-to-all(f32[16,2,128]{2,1,0:T(2,128)S(1)} %get-tuple-element.26), channel_id=1, replica_groups=mesh['zh'=4,'y'=8,'x'=4,'zl'=2,'c'=2] {'zh','zl','c'}, dimensions={0} | all-to-all | bytes 32768 | tf_op jit(solution)/shard_map/all_to_all | solution.py:364
  65.0 9.9 %all_to_all.22.gathered = f32[8,2,128]{2,1,0:T(2,128)S(1)} all-to-all(f32[8,2,128]{2,1,0:T(2,128)S(1)} %shard_map.132), channel_id=1, replica_groups=mesh['zh'=4,'y'=8,'x'=4,'zl'=2,'c'=2] {'y'}, dimensions={0} | all-to-all | bytes 16384 | tf_op jit(solution)/shard_map/all_to_all | solution.py:366
  75.0 0.0 collective-permute-done.2.arrived
  75.0 0.8 %shard_map.133 = (bf16[256,128]{1,0:T(8,128)(2,1)}, bf16[256,128]{1,0:T(8,128)(2,1)}, f32[128]{0:T(128)}, f32[128]{0:T(128)}) custom-call(f32[512,128]{1,0:T(8,128)S(1)} %get-tuple-element.24.own, bf16[512,128]{1,0:T(8,128)(2,1)S(1)} %collective-permute-done.2.arrived, bf16[256,128]{1,0:T(8,128)(2,1)S(1)} %bitcast.10, f32[128]{0:T(128)S(1)} %copy-done.4, ...), custom_call_target="tpu_custom_call" | custom-call | tf_op jit(solution)/shard_map/pallas_call | solution.py:367
  (6 shorter events, 0.0 us)
Async XLA Ops:
  0.6 16.9 %collective-permute-start = (bf16[256,128]{1,0:T(8,128)(2,1)}, bf16[256,128]{1,0:T(8,128)(2,1)S(1)}, u32[]{:S(2)}, u32[]{:S(2)}) collective-permute-start(bf16[256,128]{1,0:T(8,128)(2,1)} %bitcast.7), channel_id=1, source_target_pairs={{496,0},{0,16},{16,32},{32,48},{48,64},{64,80},{80,96},{96,112},{1... | collective-permute-start | bytes 196616 | tf_op jit(solution)/shard_map/ppermute | solution.py:325
  4.7 15.8 %collective-permute-start.1 = (bf16[256,128]{1,0:T(8,128)(2,1)}, bf16[256,128]{1,0:T(8,128)(2,1)S(1)}, u32[]{:S(2)}, u32[]{:S(2)}) collective-permute-start(bf16[256,128]{1,0:T(8,128)(2,1)} %bitcast.11), channel_id=1, source_target_pairs={{496,0},{0,16},{16,32},{32,48},{48,64},{64,80},{80,96},{96,112},{1... | collective-permute-start | bytes 196616 | tf_op jit(solution)/shard_map/ppermute | solution.py:325
  8.7 11.8 %copy-start.1 = (bf16[128,2,128]{2,1,0:T(2,128)(2,1)S(1)}, bf16[128,2,128]{2,1,0:T(2,128)(2,1)}, u32[]{:S(2)}) copy-start(bf16[128,2,128]{2,1,0:T(2,128)(2,1)} %param.10) | copy-start | bytes 196612
  8.7 11.8 %copy-start.2 = (bf16[128,2,128]{2,1,0:T(2,128)(2,1)S(1)}, bf16[128,2,128]{2,1,0:T(2,128)(2,1)}, u32[]{:S(2)}) copy-start(bf16[128,2,128]{2,1,0:T(2,128)(2,1)} %param.11) | copy-start | bytes 196612
  21.4 4.2 %copy-start = (bf16[128,16,128]{2,1,0:T(8,128)(2,1)S(1)}, bf16[128,16,128]{2,1,0:T(8,128)(2,1)}, u32[]{:S(2)}) copy-start(bf16[128,16,128]{2,1,0:T(8,128)(2,1)} %q_raw.3) | copy-start | bytes 1572868
  21.4 4.2 %copy-start.4 = (f32[128]{0:T(128)S(1)}, f32[128]{0:T(128)}, u32[]{:S(2)}) copy-start(f32[128]{0:T(128)} %k_gain.3) | copy-start | bytes 1540
  21.4 4.2 %copy-start.7 = (s32[256]{0:T(256)S(1)}, s32[256]{0:T(256)}, u32[]{:S(2)}) copy-start(s32[256]{0:T(256)} %spans.1) | copy-start | bytes 3076
  21.4 4.2 %copy-start.8 = (f32[128]{0:T(128)S(1)}, f32[128]{0:T(128)}, u32[]{:S(2)}) copy-start(f32[128]{0:T(128)} %q_gain.1) | copy-start | bytes 1540
  21.4 11.1 %all-to-all-start = ((bf16[4,512,128]{2,1,0:T(8,128)(2,1)}), bf16[4,512,128]{2,1,0:T(8,128)(2,1)S(1)}, u32[]{:S(2)}, u32[]{:S(2)}) async-start(bf16[4,512,128]{2,1,0:T(8,128)(2,1)} %shard_map.128), calls=%async_computation | async-start | bytes 1048576 | tf_op jit(solution)/shard_map/all_to_all | solution.py:347
  25.6 0.8 %copy-start.3 = (bf16[128,2,128]{2,1,0:T(2,128)(2,1)S(1)}, bf16[128,2,128]{2,1,0:T(2,128)(2,1)}, u32[]{:S(2)}) copy-start(bf16[128,2,128]{2,1,0:T(2,128)(2,1)} %param.11) | copy-start | bytes 196612
  26.4 1.0 %copy-start.5 = (bf16[128,16,128]{2,1,0:T(8,128)(2,1)S(1)}, bf16[128,16,128]{2,1,0:T(8,128)(2,1)}, u32[]{:S(2)}) copy-start(bf16[128,16,128]{2,1,0:T(8,128)(2,1)} %d_out.1) | copy-start | bytes 1572868
  27.5 1.0 %copy-start.6 = (bf16[128,16,128]{2,1,0:T(8,128)(2,1)S(1)}, bf16[128,16,128]{2,1,0:T(8,128)(2,1)}, u32[]{:S(2)}) copy-start(bf16[128,16,128]{2,1,0:T(8,128)(2,1)} %attn_out.1) | copy-start | bytes 1572868
  47.2 27.7 %collective-permute-start.2 = (bf16[512,128]{1,0:T(8,128)(2,1)S(1)}, bf16[512,128]{1,0:T(8,128)(2,1)S(1)}, u32[]{:S(2)}, u32[]{:S(2)}) collective-permute-start(bf16[512,128]{1,0:T(8,128)(2,1)S(1)} %get-tuple-element.25), channel_id=1, source_target_pairs={{16,0},{32,16},{48,32},{64,48},{80,64},{96,80},{112,96},{128,112},... | collective-permute-start | bytes 393224 | tf_op jit(solution)/shard_map/ppermute | solution.py:325

commit v4 on v3

--- a/solution.py
+++ b/solution.py
@@ -90,15 +90,14 @@
     flip, _, wrapped = facts(spans)
     flipped = flip == 1
     gain = q_gain[...].reshape(1, DH)
-    ones = jnp.ones((8, DH), F32)
+    ones = jnp.ones((8, DH), BF16)
     for group in range(KV):
         q_rows = q_raw[...].astype(F32)[:, group * MEM:(group + 1) * MEM, :]
         unit, _ = unit_of(q_rows.reshape(TOK * MEM, DH))
         normed = (unit * gain).astype(BF16)
         grads = d_out[...].astype(F32)[:, group * MEM:(group + 1) * MEM, :].reshape(TOK * MEM, DH)
         outs = attn_out[...].astype(F32)[:, group * MEM:(group + 1) * MEM, :].reshape(TOK * MEM, DH)
-        row_delta = lax.dot_general(ones, grads * outs, (((1,), (1,)), ((), ())),
-                                    precision=lax.Precision.HIGHEST, preferred_element_type=F32)
+        row_delta = sum(dot_nt(ones, term.astype(BF16)) for term in three_terms(grads * outs))
         grads = grads.astype(BF16)
         for half in range(2):
             rows = slice(half * ROWS, (half + 1) * ROWS)
@@ -169,9 +168,9 @@
             pltpu.make_async_copy(k_behind, target, sems.at[slot, which]).wait()
 
 
-def three_terms(row):
-    high = row.astype(BF16).astype(F32)
-    rest = row - high
+def three_terms(floats):
+    high = floats.astype(BF16).astype(F32)
+    rest = floats - high
     middle = rest.astype(BF16).astype(F32)
     return [high, middle, rest - middle]
 

time: 76.4 us -> 76.2 us (level)
  blocking collectives: 36.2 us -> 34.6 us
  Pallas kernels: 9.34 us -> 10.2 us
    all_to_all x1, blocking collectives: 15.8 us -> 14.6 us  [per_device(): gains = lax.all_to_all(gains, FIRST, 0, 0)]
    pallas_call x1, Pallas kernels: 4.04 us -> 5.24 us  [per_device(): call(main_kernel, [((TOK, KV * MEM, DH), BF16), ((SLOTS, PAYLOAD + EXTRA,...]
where the time goes in v4:
time: 76.2 us; the launch traced here: 75.4 us
  blocking collectives  34.6 us (45%)
  starting transfers between devices  13.3 us (17%)
  waiting for transfers between devices  12.7 us (17%)
  Pallas kernels  10.2 us (13%)
  local copies, waits for them, and re-layouts  3.19 us (4%)
    all_to_all x1, blocking collectives, per_device(): gains = lax.all_to_all(gains, FIRST, 0, 0)  14.6 us
    ppermute x3, waiting for transfers between devices, step(): lax.ppermute(block, axes, [((i - distance) % size, i) for i in range(size)])  11.6 us
    all_to_all x1, blocking collectives, per_device(): pieces = lax.all_to_all(pieces, 'x', 0, 0)  10.1 us
    all_to_all x1, blocking collectives, per_device(): gains = lax.all_to_all(gains, SECOND, 0, 0)  9.95 us
    ppermute x3, starting transfers between devices, step(): lax.ppermute(block, axes, [((i - distance) % size, i) for i in range(size)])  9.16 us
    pallas_call x1, Pallas kernels, per_device(): call(main_kernel, [((TOK, KV * MEM, DH), BF16), ((SLOTS, PAYLOAD + EXTRA,...  5.24 us
    all_to_all x1, starting transfers between devices, per_device(): blocks = lax.all_to_all(blocks, 'x', 0, 0)  4.16 us
    pallas_call x1, Pallas kernels, per_device(): call(prep_kernel, [((KV, 2, ROWS, DH), BF16), ((KV, 2, ROWS, DH), BF16),...  3.01 us
  transfers between devices with their start and end apart: 4, of which 3 were waited for; matrix products, arithmetic and copies ran while one was open for 1% of the time, Pallas kernels for 4%

profile of v4, /device:TPU:1, one launch (start us, length us, event | category | flops | bytes accessed | tf_op | source)
XLA Modules:
  0.0 75.4 jit_solution(5678213636675694238)
XLA Ops:
  0.6 4.0 %collective-permute-start = (bf16[256,128]{1,0:T(8,128)(2,1)}, bf16[256,128]{1,0:T(8,128)(2,1)S(1)}, u32[]{:S(2)}, u32[]{:S(2)}) collective-permute-start(bf16[256,128]{1,0:T(8,128)(2,1)} %bitcast.7), channel_id=1, source_target_pairs={{496,0},{0,16},{16,32},{32,48},{48,64},{64,80},{80,96},{96,112},{1... | collective-permute-start | bytes 196616 | tf_op jit(solution)/shard_map/ppermute | solution.py:324
  4.7 3.2 %collective-permute-start.1 = (bf16[256,128]{1,0:T(8,128)(2,1)}, bf16[256,128]{1,0:T(8,128)(2,1)S(1)}, u32[]{:S(2)}, u32[]{:S(2)}) collective-permute-start(bf16[256,128]{1,0:T(8,128)(2,1)} %bitcast.11), channel_id=1, source_target_pairs={{496,0},{0,16},{16,32},{32,48},{48,64},{64,80},{80,96},{96,112},{1... | collective-permute-start | bytes 196616 | tf_op jit(solution)/shard_map/ppermute | solution.py:324
  7.9 0.7 multiply_bitcast_fusion
  8.6 0.1 copy.15
  8.7 0.0 copy-start.1
  8.7 0.0 copy-start.2
  8.7 0.1 reshape.34.lse2
  8.9 8.7 %collective-permute-done.k_behind = bf16[256,128]{1,0:T(8,128)(2,1)S(1)} collective-permute-done((bf16[256,128]{1,0:T(8,128)(2,1)}, bf16[256,128]{1,0:T(8,128)(2,1)S(1)}, u32[]{:S(2)}, u32[]{:S(2)}) %collective-permute-start) | collective-permute-done | bytes 65568 | tf_op jit(solution)/shard_map/ppermute | solution.py:324
  17.6 2.9 %collective-permute-done.1.v_behind = bf16[256,128]{1,0:T(8,128)(2,1)S(1)} collective-permute-done((bf16[256,128]{1,0:T(8,128)(2,1)}, bf16[256,128]{1,0:T(8,128)(2,1)S(1)}, u32[]{:S(2)}, u32[]{:S(2)}) %collective-permute-start.1) | collective-permute-done | bytes 65568 | tf_op jit(solution)/shard_map/ppermute | solution.py:324
  20.5 0.0 copy-done.1
  20.5 0.0 copy-done.2
  20.5 0.8 %shard_map.128 = bf16[4,512,128]{2,1,0:T(8,128)(2,1)} custom-call(bf16[256,128]{1,0:T(8,128)(2,1)S(1)} %bitcast.8, bf16[256,128]{1,0:T(8,128)(2,1)S(1)} %bitcast.12, bf16[256,128]{1,0:T(8,128)(2,1)S(1)} %collective-permute-done.k_behind, bf16[256,128]{1,0:T(8,128)(2,1)S(1)} %collective-permute-done.1.v_behind), custom_call_target="tpu_custom_call" | custom-call | bytes 1048576 | tf_op jit(solution)/shard_map/pallas_call | solution.py:344
  21.4 0.0 copy-start
  21.4 0.0 copy-start.4
  21.4 0.0 copy-start.7
  21.4 0.0 copy-start.8
  21.4 4.2 %all-to-all-start = ((bf16[4,512,128]{2,1,0:T(8,128)(2,1)}), bf16[4,512,128]{2,1,0:T(8,128)(2,1)S(1)}, u32[]{:S(2)}, u32[]{:S(2)}) async-start(bf16[4,512,128]{2,1,0:T(8,128)(2,1)} %shard_map.128), calls=%async_computation | async-start | bytes 1048576 | tf_op jit(solution)/shard_map/all_to_all | solution.py:346
  25.6 0.0 copy-done
  25.6 0.0 copy-start.3
  25.6 0.8 %copy-done.3 = bf16[128,2,128]{2,1,0:T(2,128)(2,1)S(1)} copy-done((bf16[128,2,128]{2,1,0:T(2,128)(2,1)S(1)}, bf16[128,2,128]{2,1,0:T(2,128)(2,1)}, u32[]{:S(2)}) %copy-start.3) | copy-done | bytes 65560
  26.4 1.0 %copy-done.5 = bf16[128,16,128]{2,1,0:T(8,128)(2,1)S(1)} copy-done((bf16[128,16,128]{2,1,0:T(8,128)(2,1)S(1)}, bf16[128,16,128]{2,1,0:T(8,128)(2,1)}, u32[]{:S(2)}) %copy-start.5) | copy-done | bytes 524312
  27.5 1.0 %copy-done.6 = bf16[128,16,128]{2,1,0:T(8,128)(2,1)S(1)} copy-done((bf16[128,16,128]{2,1,0:T(8,128)(2,1)S(1)}, bf16[128,16,128]{2,1,0:T(8,128)(2,1)}, u32[]{:S(2)}) %copy-start.6) | copy-done | bytes 524312
  28.5 3.0 %shard_map.129 = (bf16[2,2,512,128]{3,2,1,0:T(8,128)(2,1)S(1)}, bf16[2,2,512,128]{3,2,1,0:T(8,128)(2,1)S(1)}, f32[2,2,512,128]{3,2,1,0:T(8,128)S(1)}, f32[552,128]{1,0:T(8,128)S(1)}) custom-call(s32[256]{0:T(256)S(1)} %copy-done.7, bf16[128,16,128]{2,1,0:T(8,128)(2,1)S(1)} %copy-done, bf16[128,16,128]{2,1,0:T(8,128)(2,1)S(1)} %copy-done.5, ...), custom_call_target="tpu_custom_call" | custom-call | flops 6000000000 | bytes 4194304 | tf_op jit(solution)/shard_map/pallas_call | solution.py:335
  31.5 1.0 %all-to-all-done.blocks = bf16[4,512,128]{2,1,0:T(8,128)(2,1)S(1)} async-done(((bf16[4,512,128]{2,1,0:T(8,128)(2,1)}), bf16[4,512,128]{2,1,0:T(8,128)(2,1)S(1)}, u32[]{:S(2)}, u32[]{:S(2)}) %all-to-all-start) | async-done | bytes 524320 | tf_op jit(solution)/shard_map/all_to_all | solution.py:346
  32.5 5.2 %shard_map.130 = (bf16[128,16,128]{2,1,0:T(8,128)(2,1)}, bf16[4,528,128]{2,1,0:T(8,128)(2,1)S(1)}) custom-call(bf16[4,512,128]{2,1,0:T(8,128)(2,1)S(1)} %all-to-all-done.blocks, bf16[2,2,512,128]{3,2,1,0:T(8,128)(2,1)S(1)} %get-tuple-element.18.q_norm, bf16[2,2,512,128]{3,2,1,0:T(8,128)(2,1)S(1)} %get-tuple-element.19.grads_out, ...), custom_call_target="tpu_custom_call" | custom-call | tf_op jit(solution)/shard_map/pallas_call | solution.py:347
  37.8 10.1 %all_to_all.20.pieces = bf16[4,528,128]{2,1,0:T(8,128)(2,1)S(1)} all-to-all(bf16[4,528,128]{2,1,0:T(8,128)(2,1)S(1)} %get-tuple-element.23), channel_id=1, replica_groups=mesh['zh'=4,'y'=8,'x'=4,'zl'=2,'c'=2] {'x'}, dimensions={0} | all-to-all | bytes 1081344 | tf_op jit(solution)/shard_map/all_to_all | solution.py:356
  47.9 0.2 shard_map.131
  48.1 1.9 %collective-permute-start.2 = (bf16[512,128]{1,0:T(8,128)(2,1)S(1)}, bf16[512,128]{1,0:T(8,128)(2,1)S(1)}, u32[]{:S(2)}, u32[]{:S(2)}) collective-permute-start(bf16[512,128]{1,0:T(8,128)(2,1)S(1)} %get-tuple-element.25), channel_id=1, source_target_pairs={{16,0},{32,16},{48,32},{64,48},{80,64},{96,80},{112,96},{128,112},... | collective-permute-start | bytes 393224 | tf_op jit(solution)/shard_map/ppermute | solution.py:324
  50.0 14.6 %all_to_all.21.gathered = f32[16,2,128]{2,1,0:T(2,128)S(1)} all-to-all(f32[16,2,128]{2,1,0:T(2,128)S(1)} %get-tuple-element.26), channel_id=1, replica_groups=mesh['zh'=4,'y'=8,'x'=4,'zl'=2,'c'=2] {'zh','zl','c'}, dimensions={0} | all-to-all | bytes 32768 | tf_op jit(solution)/shard_map/all_to_all | solution.py:363
  64.7 9.9 %all_to_all.22.gathered = f32[8,2,128]{2,1,0:T(2,128)S(1)} all-to-all(f32[8,2,128]{2,1,0:T(2,128)S(1)} %shard_map.132), channel_id=1, replica_groups=mesh['zh'=4,'y'=8,'x'=4,'zl'=2,'c'=2] {'y'}, dimensions={0} | all-to-all | bytes 16384 | tf_op jit(solution)/shard_map/all_to_all | solution.py:365
  74.6 0.0 collective-permute-done.2.arrived
  74.6 0.8 %shard_map.133 = (bf16[256,128]{1,0:T(8,128)(2,1)}, bf16[256,128]{1,0:T(8,128)(2,1)}, f32[128]{0:T(128)}, f32[128]{0:T(128)}) custom-call(f32[512,128]{1,0:T(8,128)S(1)} %get-tuple-element.24.own, bf16[512,128]{1,0:T(8,128)(2,1)S(1)} %collective-permute-done.2.arrived, bf16[256,128]{1,0:T(8,128)(2,1)S(1)} %bitcast.10, f32[128]{0:T(128)S(1)} %copy-done.4, ...), custom_call_target="tpu_custom_call" | custom-call | tf_op jit(solution)/shard_map/pallas_call | solution.py:366
  (6 shorter events, 0.0 us)
Async XLA Ops:
  0.6 16.9 %collective-permute-start = (bf16[256,128]{1,0:T(8,128)(2,1)}, bf16[256,128]{1,0:T(8,128)(2,1)S(1)}, u32[]{:S(2)}, u32[]{:S(2)}) collective-permute-start(bf16[256,128]{1,0:T(8,128)(2,1)} %bitcast.7), channel_id=1, source_target_pairs={{496,0},{0,16},{16,32},{32,48},{48,64},{64,80},{80,96},{96,112},{1... | collective-permute-start | bytes 196616 | tf_op jit(solution)/shard_map/ppermute | solution.py:324
  4.7 15.8 %collective-permute-start.1 = (bf16[256,128]{1,0:T(8,128)(2,1)}, bf16[256,128]{1,0:T(8,128)(2,1)S(1)}, u32[]{:S(2)}, u32[]{:S(2)}) collective-permute-start(bf16[256,128]{1,0:T(8,128)(2,1)} %bitcast.11), channel_id=1, source_target_pairs={{496,0},{0,16},{16,32},{32,48},{48,64},{64,80},{80,96},{96,112},{1... | collective-permute-start | bytes 196616 | tf_op jit(solution)/shard_map/ppermute | solution.py:324
  8.7 11.8 %copy-start.1 = (bf16[128,2,128]{2,1,0:T(2,128)(2,1)S(1)}, bf16[128,2,128]{2,1,0:T(2,128)(2,1)}, u32[]{:S(2)}) copy-start(bf16[128,2,128]{2,1,0:T(2,128)(2,1)} %param.10) | copy-start | bytes 196612
  8.7 11.8 %copy-start.2 = (bf16[128,2,128]{2,1,0:T(2,128)(2,1)S(1)}, bf16[128,2,128]{2,1,0:T(2,128)(2,1)}, u32[]{:S(2)}) copy-start(bf16[128,2,128]{2,1,0:T(2,128)(2,1)} %param.11) | copy-start | bytes 196612
  21.4 4.2 %copy-start = (bf16[128,16,128]{2,1,0:T(8,128)(2,1)S(1)}, bf16[128,16,128]{2,1,0:T(8,128)(2,1)}, u32[]{:S(2)}) copy-start(bf16[128,16,128]{2,1,0:T(8,128)(2,1)} %q_raw.3) | copy-start | bytes 1572868
  21.4 4.2 %copy-start.4 = (f32[128]{0:T(128)S(1)}, f32[128]{0:T(128)}, u32[]{:S(2)}) copy-start(f32[128]{0:T(128)} %k_gain.3) | copy-start | bytes 1540
  21.4 4.2 %copy-start.7 = (s32[256]{0:T(256)S(1)}, s32[256]{0:T(256)}, u32[]{:S(2)}) copy-start(s32[256]{0:T(256)} %spans.1) | copy-start | bytes 3076
  21.4 4.2 %copy-start.8 = (f32[128]{0:T(128)S(1)}, f32[128]{0:T(128)}, u32[]{:S(2)}) copy-start(f32[128]{0:T(128)} %q_gain.1) | copy-start | bytes 1540
  21.4 11.1 %all-to-all-start = ((bf16[4,512,128]{2,1,0:T(8,128)(2,1)}), bf16[4,512,128]{2,1,0:T(8,128)(2,1)S(1)}, u32[]{:S(2)}, u32[]{:S(2)}) async-start(bf16[4,512,128]{2,1,0:T(8,128)(2,1)} %shard_map.128), calls=%async_computation | async-start | bytes 1048576 | tf_op jit(solution)/shard_map/all_to_all | solution.py:346
  25.6 0.8 %copy-start.3 = (bf16[128,2,128]{2,1,0:T(2,128)(2,1)S(1)}, bf16[128,2,128]{2,1,0:T(2,128)(2,1)}, u32[]{:S(2)}) copy-start(bf16[128,2,128]{2,1,0:T(2,128)(2,1)} %param.11) | copy-start | bytes 196612
  26.4 1.0 %copy-start.5 = (bf16[128,16,128]{2,1,0:T(8,128)(2,1)S(1)}, bf16[128,16,128]{2,1,0:T(8,128)(2,1)}, u32[]{:S(2)}) copy-start(bf16[128,16,128]{2,1,0:T(8,128)(2,1)} %d_out.1) | copy-start | bytes 1572868
  27.5 1.0 %copy-start.6 = (bf16[128,16,128]{2,1,0:T(8,128)(2,1)S(1)}, bf16[128,16,128]{2,1,0:T(8,128)(2,1)}, u32[]{:S(2)}) copy-start(bf16[128,16,128]{2,1,0:T(8,128)(2,1)} %attn_out.1) | copy-start | bytes 1572868
  48.1 26.5 %collective-permute-start.2 = (bf16[512,128]{1,0:T(8,128)(2,1)S(1)}, bf16[512,128]{1,0:T(8,128)(2,1)S(1)}, u32[]{:S(2)}, u32[]{:S(2)}) collective-permute-start(bf16[512,128]{1,0:T(8,128)(2,1)S(1)} %get-tuple-element.25), channel_id=1, source_target_pairs={{16,0},{32,16},{48,32},{64,48},{80,64},{96,80},{112,96},{128,112},... | collective-permute-start | bytes 393224 | tf_op jit(solution)/shard_map/ppermute | solution.py:324

commit v5 on v4

--- a/solution.py
+++ b/solution.py
@@ -148,26 +148,6 @@
         [jnp.sum(made[0] * k_unit, axis=0, keepdims=True), gain, k_gain[...].reshape(1, DH)] + flags, axis=0)
 
 
-def build_kernel(k_own, v_own, k_behind, v_behind, out, sems):
-    place = lax.axis_index("x")
-    for slot in range(SLOTS):
-        for which, (own, behind) in enumerate(((k_own, k_behind), (v_own, v_behind))):
-            target = out.at[slot, pl.ds(which * TOK * KV, TOK * KV)]
-
-            @pl.when(slot > place)
-            def _():
-                pltpu.make_async_copy(own, target, sems.at[slot, which]).start()
-
-            @pl.when(slot <= place)
-            def _():
-                pltpu.make_async_copy(behind, target, sems.at[slot, which]).start()
-
-    for slot in range(SLOTS):
-        for which in range(2):
-            target = out.at[slot, pl.ds(which * TOK * KV, TOK * KV)]
-            pltpu.make_async_copy(k_behind, target, sems.at[slot, which]).wait()
-
-
 def three_terms(floats):
     high = floats.astype(BF16).astype(F32)
     rest = floats - high
@@ -229,9 +209,16 @@
             sums[group, 0] = dk
             sums[group, 1] = dv
 
-    q_sum, tokens = finish(flip, jnp.zeros((1, DH), F32))
-    early_copy = pltpu.make_async_copy(d_q_rows.at[tokens], d_q_raw.at[tokens], sems.at[0])
-    early_copy.start()
+    def leave(half):
+        copies = []
+        for part in range(4):
+            tokens = pl.ds(pl.multiple_of(half * HALF + part * 16, 16), 16)
+            copies.append(pltpu.make_async_copy(d_q_rows.at[tokens], d_q_raw.at[tokens], sems.at[half, part]))
+            copies[-1].start()
+        return copies
+
+    q_sum, _ = finish(flip, jnp.zeros((1, DH), F32))
+    copies = leave(flip)
     for group in range(KV):
         dq, dk, dv = pair(early_keys[group], early_values[group], q_norm[group, late], grads_out[group, late],
                           *stats(group, late))
@@ -247,9 +234,8 @@
             sums[group, 2] = dk
             sums[group, 3] = dv
 
-    q_sum, tokens = finish(late, q_sum)
-    late_copy = pltpu.make_async_copy(d_q_rows.at[tokens], d_q_raw.at[tokens], sems.at[1])
-    late_copy.start()
+    q_sum, _ = finish(late, q_sum)
+    copies += leave(late)
     for group in range(KV):
         for slot in range(SLOTS):
             span = slice(slot * HALF, (slot + 1) * HALF)
@@ -269,8 +255,8 @@
     extra = jnp.concatenate(terms, axis=0).astype(BF16)
     for slot in range(SLOTS):
         pieces[slot, PAYLOAD:PAYLOAD + EXTRA] = extra
-    early_copy.wait()
-    late_copy.wait()
+    for copy in copies:
+        copy.wait()
 
 
 def sum_kernel(pieces, d_local, own, behind, gains):
@@ -341,8 +327,10 @@
         flops=int(6e9), size=1 << 22,
     )(span_order, q_raw, d_out, attn_out, lse2, k_own, v_own, q_gain, k_gain)
 
-    (blocks,) = call(build_kernel, [((SLOTS, PAYLOAD, DH), BF16)], [VMEM] * 4, [pltpu.SemaphoreType.DMA((SLOTS, 2))],
-                     size=BUILD_SIZE, out_specs=[ANY])(k_own, v_own, k_behind, v_behind)
+    slot = lax.broadcasted_iota(jnp.int32, (SLOTS, PAYLOAD, DH), 0)
+    own = jnp.concatenate([k_own, v_own], axis=0)[None]
+    behind = jnp.concatenate([k_behind, v_behind], axis=0)[None]
+    blocks = jnp.where(slot > lax.axis_index("x"), own, behind)
     blocks = lax.all_to_all(blocks, "x", 0, 0)
     d_q_raw, pieces = call(
         main_kernel,
@@ -350,7 +338,7 @@
         [VMEM] * 6,
         [pltpu.VMEM((KV, 2, ROWS, DH), F32)] + [pltpu.VMEM((SLOTS, TOK * KV, DH), F32)] * 3
         + [pltpu.VMEM((2 * SLOTS, TOK * KV, DH), F32), pltpu.VMEM((KV, 4, SLOTS * HALF, DH), F32),
-           pltpu.VMEM((TOK, KV * MEM, DH), BF16), pltpu.SemaphoreType.DMA((2,))],
+           pltpu.VMEM((TOK, KV * MEM, DH), BF16), pltpu.SemaphoreType.DMA((2, 4))],
         out_specs=[ANY, VMEM],
     )(blocks, q_norm, grads_out, d_query0, q_raw, d_local)
     pieces = lax.all_to_all(pieces, "x", 0, 0)

time: 76.2 us -> 76.1 us (level)
  Pallas kernels: 10.2 us -> 8.18 us
  blocking collectives: 34.6 us -> 35.9 us
  other arithmetic: 0.7 us -> 1.81 us
    all_to_all x1, blocking collectives: 14.6 us -> 15.8 us  [per_device(): gains = lax.all_to_all(gains, FIRST, 0, 0)]
    pallas_call x1, Pallas kernels: 5.24 us -> 4.08 us  [per_device(): call(main_kernel, [((TOK, KV * MEM, DH), BF16), ((SLOTS, PAYLOAD + EXTRA,...]
    select_n x0 -> x1, other arithmetic: none -> 0.9 us  [per_device(): blocks = jnp.where(slot > lax.axis_index('x'), own, behind)]
    concatenate x0 -> x2, other arithmetic: none -> 0.9 us  [the longest x1 0.89 us: per_device(): own = jnp.concatenate([k_own, v_own], axis=0)[None]]
    pallas_call x1 -> x0, Pallas kernels: 0.85 us -> none  [per_device(): call(build_kernel, [((SLOTS, PAYLOAD, DH), BF16)], [VMEM] * 4, [pltpu.Sem...]
  transfers between devices with their start and end apart: 4 -> 4, of which waited for: 3 -> 3; matrix products, arithmetic and copies ran while one was open for 1% -> 2% of each run, Pallas kernels for 4% -> 4%
where the time goes in v5:
time: 76.1 us; the launch traced here: 75.5 us
  blocking collectives  35.9 us (47%)
  starting transfers between devices  13.3 us (17%)
  waiting for transfers between devices  12.4 us (16%)
  Pallas kernels  8.18 us (11%)
  local copies, waits for them, and re-layouts  3.18 us (4%)
  other arithmetic  1.81 us (2%)
  between operations  0.77 us (1%)
    all_to_all x1, blocking collectives, per_device(): gains = lax.all_to_all(gains, FIRST, 0, 0)  15.8 us
    ppermute x3, waiting for transfers between devices, step(): lax.ppermute(block, axes, [((i - distance) % size, i) for i in range(size)])  11.4 us
    all_to_all x1, blocking collectives, per_device(): pieces = lax.all_to_all(pieces, 'x', 0, 0)  10.1 us
    all_to_all x1, blocking collectives, per_device(): gains = lax.all_to_all(gains, SECOND, 0, 0)  9.96 us
    ppermute x3, starting transfers between devices, step(): lax.ppermute(block, axes, [((i - distance) % size, i) for i in range(size)])  9.16 us
    all_to_all x1, starting transfers between devices, per_device(): blocks = lax.all_to_all(blocks, 'x', 0, 0)  4.16 us
    pallas_call x1, Pallas kernels, per_device(): call(main_kernel, [((TOK, KV * MEM, DH), BF16), ((SLOTS, PAYLOAD + EXTRA,...  4.08 us
    pallas_call x1, Pallas kernels, per_device(): call(prep_kernel, [((KV, 2, ROWS, DH), BF16), ((KV, 2, ROWS, DH), BF16),...  3.02 us
  transfers between devices with their start and end apart: 4, of which 3 were waited for; matrix products, arithmetic and copies ran while one was open for 2% of the time, Pallas kernels for 4%

profile of v5, /device:TPU:1, one launch (start us, length us, event | category | flops | bytes accessed | tf_op | source)
XLA Modules:
  0.0 75.5 jit_solution(6049557270600908873)
XLA Ops:
  0.6 4.0 %collective-permute-start = (bf16[256,128]{1,0:T(8,128)(2,1)}, bf16[256,128]{1,0:T(8,128)(2,1)S(1)}, u32[]{:S(2)}, u32[]{:S(2)}) collective-permute-start(bf16[256,128]{1,0:T(8,128)(2,1)} %bitcast.7), channel_id=1, source_target_pairs={{496,0},{0,16},{16,32},{32,48},{48,64},{64,80},{80,96},{96,112},{1... | collective-permute-start | bytes 196616 | tf_op jit(solution)/shard_map/ppermute | solution.py:310
  4.7 3.2 %collective-permute-start.1 = (bf16[256,128]{1,0:T(8,128)(2,1)}, bf16[256,128]{1,0:T(8,128)(2,1)S(1)}, u32[]{:S(2)}, u32[]{:S(2)}) collective-permute-start(bf16[256,128]{1,0:T(8,128)(2,1)} %bitcast.11), channel_id=1, source_target_pairs={{496,0},{0,16},{16,32},{32,48},{48,64},{64,80},{80,96},{96,112},{1... | collective-permute-start | bytes 196616 | tf_op jit(solution)/shard_map/ppermute | solution.py:310
  7.9 0.0 copy-start.8
  7.9 0.9 %pad_maximum_fusion = bf16[512,128]{1,0:T(8,128)(2,1)S(1)} fusion(bf16[256,128]{1,0:T(8,128)(2,1)} %bitcast.12, bf16[256,128]{1,0:T(8,128)(2,1)} %bitcast.8), kind=kLoop, calls=%fused_computation.1 | loop fusion | flops 262144 | bytes 262144 | tf_op jit(solution)/shard_map/concatenate | solution.py:331
  8.8 0.0 copy-done.8
  8.8 0.1 copy.15
  8.9 0.1 reshape.36.lse2
  9.1 8.5 %collective-permute-done = bf16[256,128]{1,0:T(8,128)(2,1)S(1)} collective-permute-done((bf16[256,128]{1,0:T(8,128)(2,1)}, bf16[256,128]{1,0:T(8,128)(2,1)S(1)}, u32[]{:S(2)}, u32[]{:S(2)}) %collective-permute-start) | collective-permute-done | bytes 65568 | tf_op jit(solution)/shard_map/ppermute | solution.py:310
  17.6 2.9 %collective-permute-done.1 = bf16[256,128]{1,0:T(8,128)(2,1)S(1)} collective-permute-done((bf16[256,128]{1,0:T(8,128)(2,1)}, bf16[256,128]{1,0:T(8,128)(2,1)S(1)}, u32[]{:S(2)}, u32[]{:S(2)}) %collective-permute-start.1) | collective-permute-done | bytes 65568 | tf_op jit(solution)/shard_map/ppermute | solution.py:310
  20.5 0.9 %broadcast_select_fusion = bf16[4,512,128]{2,1,0:T(8,128)(2,1)} fusion(pred[4]{0:T(512)(128)(4,1)S(1)} %iota_compare_fusion, bf16[512,128]{1,0:T(8,128)(2,1)S(1)} %pad_maximum_fusion.1, bf16[512,128]{1,0:T(8,128)(2,1)S(1)} %pad_maximum_fusion), kind=kLoop, calls=%fused_computation | loop fusion | flops 262144 | bytes 786436 | tf_op jit(solution)/shard_map/jit(_where)/select_n | solution.py:333
  21.4 0.0 copy-start
  21.4 0.0 copy-start.7
  21.4 4.2 %all-to-all-start = ((bf16[4,512,128]{2,1,0:T(8,128)(2,1)}), bf16[4,512,128]{2,1,0:T(8,128)(2,1)S(1)}, u32[]{:S(2)}, u32[]{:S(2)}) async-start(bf16[4,512,128]{2,1,0:T(8,128)(2,1)} %broadcast_select_fusion), calls=%async_computation | async-start | bytes 1048576 | tf_op jit(solution)/shard_map/all_to_all | solution.py:334
  25.6 0.0 copy-done
  25.6 0.0 copy-done.1
  25.6 0.0 copy-done.3
  25.6 0.0 copy-done.6
  25.6 0.0 copy-done.7
  25.6 0.0 copy-start.2
  25.6 0.8 %copy-done.2 = bf16[128,2,128]{2,1,0:T(2,128)(2,1)S(1)} copy-done((bf16[128,2,128]{2,1,0:T(2,128)(2,1)S(1)}, bf16[128,2,128]{2,1,0:T(2,128)(2,1)}, u32[]{:S(2)}) %copy-start.2) | copy-done | bytes 65560
  26.5 1.0 %copy-done.4 = bf16[128,16,128]{2,1,0:T(8,128)(2,1)S(1)} copy-done((bf16[128,16,128]{2,1,0:T(8,128)(2,1)S(1)}, bf16[128,16,128]{2,1,0:T(8,128)(2,1)}, u32[]{:S(2)}) %copy-start.4) | copy-done | bytes 524312
  27.5 1.0 %copy-done.5 = bf16[128,16,128]{2,1,0:T(8,128)(2,1)S(1)} copy-done((bf16[128,16,128]{2,1,0:T(8,128)(2,1)S(1)}, bf16[128,16,128]{2,1,0:T(8,128)(2,1)}, u32[]{:S(2)}) %copy-start.5) | copy-done | bytes 524312
  28.6 3.0 %shard_map.128 = (bf16[2,2,512,128]{3,2,1,0:T(8,128)(2,1)S(1)}, bf16[2,2,512,128]{3,2,1,0:T(8,128)(2,1)S(1)}, f32[2,2,512,128]{3,2,1,0:T(8,128)S(1)}, f32[552,128]{1,0:T(8,128)S(1)}) custom-call(s32[256]{0:T(256)S(1)} %copy-done.6, bf16[128,16,128]{2,1,0:T(8,128)(2,1)S(1)} %copy-done, bf16[128,16,128]{2,1,0:T(8,128)(2,1)S(1)} %copy-done.4, ...), custom_call_target="tpu_custom_call" | custom-call | flops 6000000000 | bytes 4194304 | tf_op jit(solution)/shard_map/pallas_call | solution.py:321
  31.6 1.0 %all-to-all-done.blocks = bf16[4,512,128]{2,1,0:T(8,128)(2,1)S(1)} async-done(((bf16[4,512,128]{2,1,0:T(8,128)(2,1)}), bf16[4,512,128]{2,1,0:T(8,128)(2,1)S(1)}, u32[]{:S(2)}, u32[]{:S(2)}) %all-to-all-start) | async-done | bytes 524320 | tf_op jit(solution)/shard_map/all_to_all | solution.py:334
  32.6 4.1 %shard_map.129 = (bf16[128,16,128]{2,1,0:T(8,128)(2,1)}, bf16[4,528,128]{2,1,0:T(8,128)(2,1)S(1)}) custom-call(bf16[4,512,128]{2,1,0:T(8,128)(2,1)S(1)} %all-to-all-done.blocks, bf16[2,2,512,128]{3,2,1,0:T(8,128)(2,1)S(1)} %get-tuple-element.18.q_norm, bf16[2,2,512,128]{3,2,1,0:T(8,128)(2,1)S(1)} %get-tuple-element.19.grads_out, ...), custom_call_target="tpu_custom_call" | custom-call | tf_op jit(solution)/shard_map/pallas_call | solution.py:335
  36.7 10.1 %all_to_all.20.pieces = bf16[4,528,128]{2,1,0:T(8,128)(2,1)S(1)} all-to-all(bf16[4,528,128]{2,1,0:T(8,128)(2,1)S(1)} %get-tuple-element.23), channel_id=1, replica_groups=mesh['zh'=4,'y'=8,'x'=4,'zl'=2,'c'=2] {'x'}, dimensions={0} | all-to-all | bytes 1081344 | tf_op jit(solution)/shard_map/all_to_all | solution.py:344
  46.8 0.2 shard_map.130
  47.0 1.9 %collective-permute-start.2 = (bf16[512,128]{1,0:T(8,128)(2,1)S(1)}, bf16[512,128]{1,0:T(8,128)(2,1)S(1)}, u32[]{:S(2)}, u32[]{:S(2)}) collective-permute-start(bf16[512,128]{1,0:T(8,128)(2,1)S(1)} %get-tuple-element.25), channel_id=1, source_target_pairs={{16,0},{32,16},{48,32},{64,48},{80,64},{96,80},{112,96},{128,112},... | collective-permute-start | bytes 393224 | tf_op jit(solution)/shard_map/ppermute | solution.py:310
  48.9 15.8 %all_to_all.21.gathered = f32[16,2,128]{2,1,0:T(2,128)S(1)} all-to-all(f32[16,2,128]{2,1,0:T(2,128)S(1)} %get-tuple-element.26), channel_id=1, replica_groups=mesh['zh'=4,'y'=8,'x'=4,'zl'=2,'c'=2] {'zh','zl','c'}, dimensions={0} | all-to-all | bytes 32768 | tf_op jit(solution)/shard_map/all_to_all | solution.py:351
  64.7 10.0 %all_to_all.22.gathered = f32[8,2,128]{2,1,0:T(2,128)S(1)} all-to-all(f32[8,2,128]{2,1,0:T(2,128)S(1)} %shard_map.131), channel_id=1, replica_groups=mesh['zh'=4,'y'=8,'x'=4,'zl'=2,'c'=2] {'y'}, dimensions={0} | all-to-all | bytes 16384 | tf_op jit(solution)/shard_map/all_to_all | solution.py:353
  74.7 0.0 collective-permute-done.2.arrived
  74.7 0.8 %shard_map.132 = (bf16[256,128]{1,0:T(8,128)(2,1)}, bf16[256,128]{1,0:T(8,128)(2,1)}, f32[128]{0:T(128)}, f32[128]{0:T(128)}) custom-call(f32[512,128]{1,0:T(8,128)S(1)} %get-tuple-element.24.own, bf16[512,128]{1,0:T(8,128)(2,1)S(1)} %collective-permute-done.2.arrived, bf16[256,128]{1,0:T(8,128)(2,1)S(1)} %bitcast.10, f32[128]{0:T(128)S(1)} %copy-done.3, ...), custom_call_target="tpu_custom_call" | custom-call | tf_op jit(solution)/shard_map/pallas_call | solution.py:354
  (9 shorter events, 0.0 us)
Async XLA Ops:
  0.6 16.9 %collective-permute-start = (bf16[256,128]{1,0:T(8,128)(2,1)}, bf16[256,128]{1,0:T(8,128)(2,1)S(1)}, u32[]{:S(2)}, u32[]{:S(2)}) collective-permute-start(bf16[256,128]{1,0:T(8,128)(2,1)} %bitcast.7), channel_id=1, source_target_pairs={{496,0},{0,16},{16,32},{32,48},{48,64},{64,80},{80,96},{96,112},{1... | collective-permute-start | bytes 196616 | tf_op jit(solution)/shard_map/ppermute | solution.py:310
  4.7 15.8 %collective-permute-start.1 = (bf16[256,128]{1,0:T(8,128)(2,1)}, bf16[256,128]{1,0:T(8,128)(2,1)S(1)}, u32[]{:S(2)}, u32[]{:S(2)}) collective-permute-start(bf16[256,128]{1,0:T(8,128)(2,1)} %bitcast.11), channel_id=1, source_target_pairs={{496,0},{0,16},{16,32},{32,48},{48,64},{64,80},{80,96},{96,112},{1... | collective-permute-start | bytes 196616 | tf_op jit(solution)/shard_map/ppermute | solution.py:310
  7.9 0.9 %copy-start.8 = (f32[16,128]{1,0:T(8,128)S(1)}, f32[16,128]{1,0:T(8,128)}, u32[]{:S(2)}) copy-start(f32[16,128]{1,0:T(8,128)} %param.14) | copy-start | bytes 24580
  21.4 4.2 %copy-start = (bf16[128,16,128]{2,1,0:T(8,128)(2,1)S(1)}, bf16[128,16,128]{2,1,0:T(8,128)(2,1)}, u32[]{:S(2)}) copy-start(bf16[128,16,128]{2,1,0:T(8,128)(2,1)} %q_raw.3) | copy-start | bytes 1572868
  21.4 4.2 %copy-start.1 = (bf16[128,2,128]{2,1,0:T(2,128)(2,1)S(1)}, bf16[128,2,128]{2,1,0:T(2,128)(2,1)}, u32[]{:S(2)}) copy-start(bf16[128,2,128]{2,1,0:T(2,128)(2,1)} %param.10) | copy-start | bytes 196612
  21.4 4.2 %copy-start.3 = (f32[128]{0:T(128)S(1)}, f32[128]{0:T(128)}, u32[]{:S(2)}) copy-start(f32[128]{0:T(128)} %k_gain.3) | copy-start | bytes 1540
  21.4 4.2 %copy-start.6 = (s32[256]{0:T(256)S(1)}, s32[256]{0:T(256)}, u32[]{:S(2)}) copy-start(s32[256]{0:T(256)} %spans.1) | copy-start | bytes 3076
  21.4 4.2 %copy-start.7 = (f32[128]{0:T(128)S(1)}, f32[128]{0:T(128)}, u32[]{:S(2)}) copy-start(f32[128]{0:T(128)} %q_gain.1) | copy-start | bytes 1540
  21.4 11.1 %all-to-all-start = ((bf16[4,512,128]{2,1,0:T(8,128)(2,1)}), bf16[4,512,128]{2,1,0:T(8,128)(2,1)S(1)}, u32[]{:S(2)}, u32[]{:S(2)}) async-start(bf16[4,512,128]{2,1,0:T(8,128)(2,1)} %broadcast_select_fusion), calls=%async_computation | async-start | bytes 1048576 | tf_op jit(solution)/shard_map/all_to_all | solution.py:334
  25.6 0.8 %copy-start.2 = (bf16[128,2,128]{2,1,0:T(2,128)(2,1)S(1)}, bf16[128,2,128]{2,1,0:T(2,128)(2,1)}, u32[]{:S(2)}) copy-start(bf16[128,2,128]{2,1,0:T(2,128)(2,1)} %param.11) | copy-start | bytes 196612
  26.5 1.0 %copy-start.4 = (bf16[128,16,128]{2,1,0:T(8,128)(2,1)S(1)}, bf16[128,16,128]{2,1,0:T(8,128)(2,1)}, u32[]{:S(2)}) copy-start(bf16[128,16,128]{2,1,0:T(8,128)(2,1)} %d_out.1) | copy-start | bytes 1572868
  27.5 1.0 %copy-start.5 = (bf16[128,16,128]{2,1,0:T(8,128)(2,1)S(1)}, bf16[128,16,128]{2,1,0:T(8,128)(2,1)}, u32[]{:S(2)}) copy-start(bf16[128,16,128]{2,1,0:T(8,128)(2,1)} %attn_out.1) | copy-start | bytes 1572868
  47.0 27.7 %collective-permute-start.2 = (bf16[512,128]{1,0:T(8,128)(2,1)S(1)}, bf16[512,128]{1,0:T(8,128)(2,1)S(1)}, u32[]{:S(2)}, u32[]{:S(2)}) collective-permute-start(bf16[512,128]{1,0:T(8,128)(2,1)S(1)} %get-tuple-element.25), channel_id=1, source_target_pairs={{16,0},{32,16},{48,32},{64,48},{80,64},{96,80},{112,96},{128,112},... | collective-permute-start | bytes 393224 | tf_op jit(solution)/shard_map/ppermute | solution.py:310

commit v6 on v4

--- a/solution.py
+++ b/solution.py
@@ -22,8 +22,8 @@
 EXTRA = 16
 BUILD_SIZE = 1 << 20
 STATS = PAYLOAD + 8
-FIRST = ("zh", "zl", "c")
-SECOND = ("y",)
+FIRST = ("y", "c")
+SECOND = ("zh", "zl")
 ANY = pl.BlockSpec(memory_space=pl.ANY)
 VMEM = pl.BlockSpec(memory_space=pltpu.VMEM)
 SMEM = pl.BlockSpec(memory_space=pltpu.SMEM)

time: 76.2 us -> 76 us (level)
  Pallas kernels: 10.2 us -> 8.98 us
  blocking collectives: 34.6 us -> 35.8 us
    all_to_all x1, blocking collectives: 9.95 us -> 11.4 us  [per_device(): gains = lax.all_to_all(gains, SECOND, 0, 0)]
    pallas_call x1, Pallas kernels: 5.24 us -> 4.04 us  [per_device(): call(main_kernel, [((TOK, KV * MEM, DH), BF16), ((SLOTS, PAYLOAD + EXTRA,...]
where the time goes in v6:
time: 76 us; the launch traced here: 75.4 us
  blocking collectives  35.8 us (47%)
  starting transfers between devices  13.3 us (18%)
  waiting for transfers between devices  12.7 us (17%)
  Pallas kernels  8.98 us (12%)
  local copies, waits for them, and re-layouts  3.19 us (4%)
  between operations  0.76 us (1%)
    all_to_all x1, blocking collectives, per_device(): gains = lax.all_to_all(gains, FIRST, 0, 0)  14.4 us
    ppermute x3, waiting for transfers between devices, step(): lax.ppermute(block, axes, [((i - distance) % size, i) for i in range(size)])  11.6 us
    all_to_all x1, blocking collectives, per_device(): gains = lax.all_to_all(gains, SECOND, 0, 0)  11.4 us
    all_to_all x1, blocking collectives, per_device(): pieces = lax.all_to_all(pieces, 'x', 0, 0)  10.1 us
    ppermute x3, starting transfers between devices, step(): lax.ppermute(block, axes, [((i - distance) % size, i) for i in range(size)])  9.16 us
    all_to_all x1, starting transfers between devices, per_device(): blocks = lax.all_to_all(blocks, 'x', 0, 0)  4.16 us
    pallas_call x1, Pallas kernels, per_device(): call(main_kernel, [((TOK, KV * MEM, DH), BF16), ((SLOTS, PAYLOAD + EXTRA,...  4.04 us
    pallas_call x1, Pallas kernels, per_device(): call(prep_kernel, [((KV, 2, ROWS, DH), BF16), ((KV, 2, ROWS, DH), BF16),...  3.01 us
  transfers between devices with their start and end apart: 4, of which 3 were waited for; matrix products, arithmetic and copies ran while one was open for 1% of the time, Pallas kernels for 4%

profile of v6, /device:TPU:1, one launch (start us, length us, event | category | flops | bytes accessed | tf_op | source)
XLA Modules:
  0.0 75.4 jit_solution(13789859999114850138)
XLA Ops:
  0.6 4.0 %collective-permute-start = (bf16[256,128]{1,0:T(8,128)(2,1)}, bf16[256,128]{1,0:T(8,128)(2,1)S(1)}, u32[]{:S(2)}, u32[]{:S(2)}) collective-permute-start(bf16[256,128]{1,0:T(8,128)(2,1)} %bitcast.7), channel_id=1, source_target_pairs={{496,0},{0,16},{16,32},{32,48},{48,64},{64,80},{80,96},{96,112},{1... | collective-permute-start | bytes 196616 | tf_op jit(solution)/shard_map/ppermute | solution.py:324
  4.7 3.2 %collective-permute-start.1 = (bf16[256,128]{1,0:T(8,128)(2,1)}, bf16[256,128]{1,0:T(8,128)(2,1)S(1)}, u32[]{:S(2)}, u32[]{:S(2)}) collective-permute-start(bf16[256,128]{1,0:T(8,128)(2,1)} %bitcast.11), channel_id=1, source_target_pairs={{496,0},{0,16},{16,32},{32,48},{48,64},{64,80},{80,96},{96,112},{1... | collective-permute-start | bytes 196616 | tf_op jit(solution)/shard_map/ppermute | solution.py:324
  7.9 0.7 multiply_bitcast_fusion
  8.6 0.1 copy.15
  8.7 0.0 copy-start.1
  8.7 0.0 copy-start.2
  8.7 0.1 reshape.34.lse2
  8.9 8.7 %collective-permute-done.k_behind = bf16[256,128]{1,0:T(8,128)(2,1)S(1)} collective-permute-done((bf16[256,128]{1,0:T(8,128)(2,1)}, bf16[256,128]{1,0:T(8,128)(2,1)S(1)}, u32[]{:S(2)}, u32[]{:S(2)}) %collective-permute-start) | collective-permute-done | bytes 65568 | tf_op jit(solution)/shard_map/ppermute | solution.py:324
  17.6 2.9 %collective-permute-done.1.v_behind = bf16[256,128]{1,0:T(8,128)(2,1)S(1)} collective-permute-done((bf16[256,128]{1,0:T(8,128)(2,1)}, bf16[256,128]{1,0:T(8,128)(2,1)S(1)}, u32[]{:S(2)}, u32[]{:S(2)}) %collective-permute-start.1) | collective-permute-done | bytes 65568 | tf_op jit(solution)/shard_map/ppermute | solution.py:324
  20.5 0.0 copy-done.1
  20.5 0.0 copy-done.2
  20.5 0.8 %shard_map.128 = bf16[4,512,128]{2,1,0:T(8,128)(2,1)} custom-call(bf16[256,128]{1,0:T(8,128)(2,1)S(1)} %bitcast.8, bf16[256,128]{1,0:T(8,128)(2,1)S(1)} %bitcast.12, bf16[256,128]{1,0:T(8,128)(2,1)S(1)} %collective-permute-done.k_behind, bf16[256,128]{1,0:T(8,128)(2,1)S(1)} %collective-permute-done.1.v_behind), custom_call_target="tpu_custom_call" | custom-call | bytes 1048576 | tf_op jit(solution)/shard_map/pallas_call | solution.py:344
  21.4 0.0 copy-start
  21.4 0.0 copy-start.4
  21.4 0.0 copy-start.7
  21.4 0.0 copy-start.8
  21.4 4.2 %all-to-all-start = ((bf16[4,512,128]{2,1,0:T(8,128)(2,1)}), bf16[4,512,128]{2,1,0:T(8,128)(2,1)S(1)}, u32[]{:S(2)}, u32[]{:S(2)}) async-start(bf16[4,512,128]{2,1,0:T(8,128)(2,1)} %shard_map.128), calls=%async_computation | async-start | bytes 1048576 | tf_op jit(solution)/shard_map/all_to_all | solution.py:346
  25.6 0.0 copy-done
  25.6 0.0 copy-start.3
  25.6 0.8 %copy-done.3 = bf16[128,2,128]{2,1,0:T(2,128)(2,1)S(1)} copy-done((bf16[128,2,128]{2,1,0:T(2,128)(2,1)S(1)}, bf16[128,2,128]{2,1,0:T(2,128)(2,1)}, u32[]{:S(2)}) %copy-start.3) | copy-done | bytes 65560
  26.4 1.0 %copy-done.5 = bf16[128,16,128]{2,1,0:T(8,128)(2,1)S(1)} copy-done((bf16[128,16,128]{2,1,0:T(8,128)(2,1)S(1)}, bf16[128,16,128]{2,1,0:T(8,128)(2,1)}, u32[]{:S(2)}) %copy-start.5) | copy-done | bytes 524312
  27.5 1.0 %copy-done.6 = bf16[128,16,128]{2,1,0:T(8,128)(2,1)S(1)} copy-done((bf16[128,16,128]{2,1,0:T(8,128)(2,1)S(1)}, bf16[128,16,128]{2,1,0:T(8,128)(2,1)}, u32[]{:S(2)}) %copy-start.6) | copy-done | bytes 524312
  28.5 3.0 %shard_map.129 = (bf16[2,2,512,128]{3,2,1,0:T(8,128)(2,1)S(1)}, bf16[2,2,512,128]{3,2,1,0:T(8,128)(2,1)S(1)}, f32[2,2,512,128]{3,2,1,0:T(8,128)S(1)}, f32[552,128]{1,0:T(8,128)S(1)}) custom-call(s32[256]{0:T(256)S(1)} %copy-done.7, bf16[128,16,128]{2,1,0:T(8,128)(2,1)S(1)} %copy-done, bf16[128,16,128]{2,1,0:T(8,128)(2,1)S(1)} %copy-done.5, ...), custom_call_target="tpu_custom_call" | custom-call | flops 6000000000 | bytes 4194304 | tf_op jit(solution)/shard_map/pallas_call | solution.py:335
  31.5 1.0 %all-to-all-done.blocks = bf16[4,512,128]{2,1,0:T(8,128)(2,1)S(1)} async-done(((bf16[4,512,128]{2,1,0:T(8,128)(2,1)}), bf16[4,512,128]{2,1,0:T(8,128)(2,1)S(1)}, u32[]{:S(2)}, u32[]{:S(2)}) %all-to-all-start) | async-done | bytes 524320 | tf_op jit(solution)/shard_map/all_to_all | solution.py:346
  32.5 4.0 %shard_map.130 = (bf16[128,16,128]{2,1,0:T(8,128)(2,1)}, bf16[4,528,128]{2,1,0:T(8,128)(2,1)S(1)}) custom-call(bf16[4,512,128]{2,1,0:T(8,128)(2,1)S(1)} %all-to-all-done.blocks, bf16[2,2,512,128]{3,2,1,0:T(8,128)(2,1)S(1)} %get-tuple-element.18.q_norm, bf16[2,2,512,128]{3,2,1,0:T(8,128)(2,1)S(1)} %get-tuple-element.19.grads_out, ...), custom_call_target="tpu_custom_call" | custom-call | tf_op jit(solution)/shard_map/pallas_call | solution.py:347
  36.6 10.1 %all_to_all.20.pieces = bf16[4,528,128]{2,1,0:T(8,128)(2,1)S(1)} all-to-all(bf16[4,528,128]{2,1,0:T(8,128)(2,1)S(1)} %get-tuple-element.23), channel_id=1, replica_groups=mesh['zh'=4,'y'=8,'x'=4,'zl'=2,'c'=2] {'x'}, dimensions={0} | all-to-all | bytes 1081344 | tf_op jit(solution)/shard_map/all_to_all | solution.py:356
  46.7 0.2 shard_map.131
  46.9 1.9 %collective-permute-start.2 = (bf16[512,128]{1,0:T(8,128)(2,1)S(1)}, bf16[512,128]{1,0:T(8,128)(2,1)S(1)}, u32[]{:S(2)}, u32[]{:S(2)}) collective-permute-start(bf16[512,128]{1,0:T(8,128)(2,1)S(1)} %get-tuple-element.25), channel_id=1, source_target_pairs={{16,0},{32,16},{48,32},{64,48},{80,64},{96,80},{112,96},{128,112},... | collective-permute-start | bytes 393224 | tf_op jit(solution)/shard_map/ppermute | solution.py:324
  48.8 14.4 %all_to_all.21.gathered = f32[16,2,128]{2,1,0:T(2,128)S(1)} all-to-all(f32[16,2,128]{2,1,0:T(2,128)S(1)} %get-tuple-element.26), channel_id=1, replica_groups=mesh['zh'=4,'y'=8,'x'=4,'zl'=2,'c'=2] {'y','c'}, dimensions={0} | all-to-all | bytes 32768 | tf_op jit(solution)/shard_map/all_to_all | solution.py:363
  63.2 11.4 %all_to_all.22.gathered = f32[8,2,128]{2,1,0:T(2,128)S(1)} all-to-all(f32[8,2,128]{2,1,0:T(2,128)S(1)} %shard_map.132), channel_id=1, replica_groups=mesh['zh'=4,'y'=8,'x'=4,'zl'=2,'c'=2] {'zh','zl'}, dimensions={0} | all-to-all | bytes 16384 | tf_op jit(solution)/shard_map/all_to_all | solution.py:365
  74.6 0.0 collective-permute-done.2.arrived
  74.6 0.8 %shard_map.133 = (bf16[256,128]{1,0:T(8,128)(2,1)}, bf16[256,128]{1,0:T(8,128)(2,1)}, f32[128]{0:T(128)}, f32[128]{0:T(128)}) custom-call(f32[512,128]{1,0:T(8,128)S(1)} %get-tuple-element.24.own, bf16[512,128]{1,0:T(8,128)(2,1)S(1)} %collective-permute-done.2.arrived, bf16[256,128]{1,0:T(8,128)(2,1)S(1)} %bitcast.10, f32[128]{0:T(128)S(1)} %copy-done.4, ...), custom_call_target="tpu_custom_call" | custom-call | tf_op jit(solution)/shard_map/pallas_call | solution.py:366
  (6 shorter events, 0.0 us)
Async XLA Ops:
  0.6 16.9 %collective-permute-start = (bf16[256,128]{1,0:T(8,128)(2,1)}, bf16[256,128]{1,0:T(8,128)(2,1)S(1)}, u32[]{:S(2)}, u32[]{:S(2)}) collective-permute-start(bf16[256,128]{1,0:T(8,128)(2,1)} %bitcast.7), channel_id=1, source_target_pairs={{496,0},{0,16},{16,32},{32,48},{48,64},{64,80},{80,96},{96,112},{1... | collective-permute-start | bytes 196616 | tf_op jit(solution)/shard_map/ppermute | solution.py:324
  4.7 15.8 %collective-permute-start.1 = (bf16[256,128]{1,0:T(8,128)(2,1)}, bf16[256,128]{1,0:T(8,128)(2,1)S(1)}, u32[]{:S(2)}, u32[]{:S(2)}) collective-permute-start(bf16[256,128]{1,0:T(8,128)(2,1)} %bitcast.11), channel_id=1, source_target_pairs={{496,0},{0,16},{16,32},{32,48},{48,64},{64,80},{80,96},{96,112},{1... | collective-permute-start | bytes 196616 | tf_op jit(solution)/shard_map/ppermute | solution.py:324
  8.7 11.8 %copy-start.1 = (bf16[128,2,128]{2,1,0:T(2,128)(2,1)S(1)}, bf16[128,2,128]{2,1,0:T(2,128)(2,1)}, u32[]{:S(2)}) copy-start(bf16[128,2,128]{2,1,0:T(2,128)(2,1)} %param.10) | copy-start | bytes 196612
  8.7 11.8 %copy-start.2 = (bf16[128,2,128]{2,1,0:T(2,128)(2,1)S(1)}, bf16[128,2,128]{2,1,0:T(2,128)(2,1)}, u32[]{:S(2)}) copy-start(bf16[128,2,128]{2,1,0:T(2,128)(2,1)} %param.11) | copy-start | bytes 196612
  21.4 4.2 %copy-start = (bf16[128,16,128]{2,1,0:T(8,128)(2,1)S(1)}, bf16[128,16,128]{2,1,0:T(8,128)(2,1)}, u32[]{:S(2)}) copy-start(bf16[128,16,128]{2,1,0:T(8,128)(2,1)} %q_raw.3) | copy-start | bytes 1572868
  21.4 4.2 %copy-start.4 = (f32[128]{0:T(128)S(1)}, f32[128]{0:T(128)}, u32[]{:S(2)}) copy-start(f32[128]{0:T(128)} %k_gain.3) | copy-start | bytes 1540
  21.4 4.2 %copy-start.7 = (s32[256]{0:T(256)S(1)}, s32[256]{0:T(256)}, u32[]{:S(2)}) copy-start(s32[256]{0:T(256)} %spans.1) | copy-start | bytes 3076
  21.4 4.2 %copy-start.8 = (f32[128]{0:T(128)S(1)}, f32[128]{0:T(128)}, u32[]{:S(2)}) copy-start(f32[128]{0:T(128)} %q_gain.1) | copy-start | bytes 1540
  21.4 11.1 %all-to-all-start = ((bf16[4,512,128]{2,1,0:T(8,128)(2,1)}), bf16[4,512,128]{2,1,0:T(8,128)(2,1)S(1)}, u32[]{:S(2)}, u32[]{:S(2)}) async-start(bf16[4,512,128]{2,1,0:T(8,128)(2,1)} %shard_map.128), calls=%async_computation | async-start | bytes 1048576 | tf_op jit(solution)/shard_map/all_to_all | solution.py:346
  25.6 0.8 %copy-start.3 = (bf16[128,2,128]{2,1,0:T(2,128)(2,1)S(1)}, bf16[128,2,128]{2,1,0:T(2,128)(2,1)}, u32[]{:S(2)}) copy-start(bf16[128,2,128]{2,1,0:T(2,128)(2,1)} %param.11) | copy-start | bytes 196612
  26.4 1.0 %copy-start.5 = (bf16[128,16,128]{2,1,0:T(8,128)(2,1)S(1)}, bf16[128,16,128]{2,1,0:T(8,128)(2,1)}, u32[]{:S(2)}) copy-start(bf16[128,16,128]{2,1,0:T(8,128)(2,1)} %d_out.1) | copy-start | bytes 1572868
  27.5 1.0 %copy-start.6 = (bf16[128,16,128]{2,1,0:T(8,128)(2,1)S(1)}, bf16[128,16,128]{2,1,0:T(8,128)(2,1)}, u32[]{:S(2)}) copy-start(bf16[128,16,128]{2,1,0:T(8,128)(2,1)} %attn_out.1) | copy-start | bytes 1572868
  46.9 27.7 %collective-permute-start.2 = (bf16[512,128]{1,0:T(8,128)(2,1)S(1)}, bf16[512,128]{1,0:T(8,128)(2,1)S(1)}, u32[]{:S(2)}, u32[]{:S(2)}) collective-permute-start(bf16[512,128]{1,0:T(8,128)(2,1)S(1)} %get-tuple-element.25), channel_id=1, source_target_pairs={{16,0},{32,16},{48,32},{64,48},{80,64},{96,80},{112,96},{128,112},... | collective-permute-start | bytes 393224 | tf_op jit(solution)/shard_map/ppermute | solution.py:324
